TPU v7x, 32 devices: a whole 2x2x4 slice. The times are simulated.
32 devices in a mesh: grp: 8 (over z, y), blk: 4 (over x, core).
Axes of the slice: x: 2, y: 2, z: 4, core: 2. Of those that a mesh axis runs over, the one named last changes fastest.
Arguments:
- features: bfloat16 [16384, 256], P(('grp', 'blk')), may hold values from -6 to 6
- d_out: float32 [16384, 256], P(('grp', 'blk')), may hold values from -6 to 6
- bucket_batch: int32 [8], P('grp'), may hold values from 1 to 2, as said below
- valid_len: int32 [8, 2], P('grp'), may hold values from 0 to 2048, as said below
- time_start: int32 [8, 2], P('grp'), may hold values from 0 to 983
- time_width: int32 [8, 2], P('grp'), may hold values from 0 to 40
- freq_start: int32 [8, 2], P('grp'), may hold values from 0 to 228
- freq_width: int32 [8, 2], P('grp'), may hold values from 0 to 27
- gains: float32 [5, 256], replicated, may hold values from 0.5 to 1.5
- inner_gain: float32 [512], replicated, may hold values from 0.5 to 1.5
- ffn1_in: bfloat16 [256, 1024], replicated, may hold values from -0.375 to 0.375
- ffn1_out: bfloat16 [1024, 256], replicated, may hold values from -0.375 to 0.375
- qkv_w: bfloat16 [256, 768], replicated, may hold values from -0.375 to 0.375
- out_w: bfloat16 [256, 256], replicated, may hold values from -6 to 6
- cg_up: bfloat16 [256, 1024], replicated, may hold values from -0.375 to 0.375
- cg_conv: bfloat16 [31, 512], replicated, may hold values from -1 to 1
- cg_down: bfloat16 [512, 256], replicated, may hold values from -0.25 to 0.25
- merge_conv: bfloat16 [31, 512], replicated, may hold values from -1 to 1
- merge_w: bfloat16 [512, 256], replicated, may hold values from -0.25 to 0.25
- ffn2_in: bfloat16 [256, 1024], replicated, may hold values from -0.375 to 0.375
- ffn2_out: bfloat16 [1024, 256], replicated, may hold values from -0.375 to 0.375
Outputs:
- out: bfloat16 [16384, 256], P(('grp', 'blk'))
- d_features: float32 [16384, 256], P(('grp', 'blk'))
- grad_gains: float32 [5, 256], replicated
- grad_inner_gain: float32 [512], replicated
- grad_ffn1_in: float32 [256, 1024], replicated
- grad_ffn1_out: float32 [1024, 256], replicated
- grad_qkv_w: float32 [256, 768], replicated
- grad_out_w: float32 [256, 256], replicated
- grad_cg_up: float32 [256, 1024], replicated
- grad_cg_conv: float32 [31, 512], replicated
- grad_cg_down: float32 [512, 256], replicated
- grad_merge_conv: float32 [31, 512], replicated
- grad_merge_w: float32 [512, 256], replicated
- grad_ffn2_in: float32 [256, 1024], replicated
- grad_ffn2_out: float32 [1024, 256], replicated
Inputs may be any that keep to these rules, and one draw needn't show every extreme that they name: Number of utterances in bucket g; its padded length is 2048 / bucket_batch[g]. Both 1 and 2 occur in every draw. `valid_len`: for a slot u below the bucket's batch size: between a quarter of the padded length and all of it, one slot of every bucket exactly the padded length. Slots at or above the batch size hold 0.
All inputs are finite; a program needn't handle non-finite values.
Results may differ from a plain program's by a relative error of at most 0.015.
Values may be sent and summed in bfloat16 or wider, within the bound.
No kernel may reach another device: no remote copies, remote signals or barrier semaphores. Data moves between devices by JAX's collectives and lax.ppermute only.
A program may use at most 128 MiB of HBM per device.

v0:
```python
import math

import jax
import jax.numpy as jnp
from jax import lax
from jax.sharding import PartitionSpec as P

HEADS = 4
HEAD_DIM = 64
BMAX = 2


LOG_BASE = 1.4426950408889634
EPSILON = 1e-05
MASKED_SCORE = -1e30


def shifted(block, axis, distance):
    devices = range(lax.axis_size(axis))
    route = [((i - distance) % len(devices), i) for i in devices]
    return lax.ppermute(block, axis, route)


def padded(shard, sides, width):
    for axis, dim in sides:
        count, length = (lax.axis_size(axis), shard.shape[dim])
        up = [(i, (i + 1) % count) for i in range(count - 1)]
        down = [(j, i) for i, j in up]
        last = lax.slice_in_dim(shard, length - width, length, axis=dim)
        leading = lax.slice_in_dim(shard, 0, width, axis=dim)
        before = lax.ppermute(last, axis, up)
        after = lax.ppermute(leading, axis, down)
        shard = jnp.concatenate([before, shard, after], axis=dim)
    return shard


def lookup(entries, indices):
    slot_ids = jnp.arange(entries.shape[0], dtype=jnp.int32)
    return jnp.sum(jnp.where(indices[:, None] == slot_ids[None, :], entries[None, :], 0), 1)


def to_half(value):
    return value.astype(jnp.bfloat16)


def product(left, right):
    return jnp.dot(left, right, preferred_element_type=jnp.float32)


def product_t(left, right):
    return lax.dot_general(
        left, right, (((1,), (1,)), ((), ())), preferred_element_type=jnp.float32
    )


def weight_grad(left, right):
    return lax.dot_general(
        left, right, (((0,), (0,)), ((), ())), preferred_element_type=jnp.float32
    )


def norm_forward(inputs, gain):
    center = inputs - jnp.mean(inputs, -1, keepdims=True)
    factor = lax.rsqrt(jnp.mean(center * center, -1, keepdims=True) + EPSILON)
    unit_part = center * factor
    return (unit_part * gain, unit_part, factor)


def norm_backward(upstream, unit_part, factor, gain):
    gain_grad = jnp.sum(upstream * unit_part, 0)
    scaled_grad = upstream * gain
    grad_in = factor * (
        scaled_grad
        - jnp.mean(scaled_grad, -1, keepdims=True)
        - unit_part * jnp.mean(scaled_grad * unit_part, -1, keepdims=True)
    )
    return (grad_in, gain_grad)


def rotate(inputs, position, direction):
    row_count = inputs.shape[0]
    half_dim = HEAD_DIM // 2
    frequency = jnp.exp(
        jnp.arange(half_dim, dtype=jnp.float32) * (-2.0 * math.log(10000.0) / HEAD_DIM)
    )
    angles = position.astype(jnp.float32)[:, None] * frequency[None, :]
    cosine = jnp.cos(angles)[:, None, :]
    sine_part = direction * jnp.sin(angles)[:, None, :]
    pairs_view = inputs.reshape(row_count, HEADS, 2, half_dim)
    former = pairs_view[:, :, 0]
    latter = pairs_view[:, :, 1]
    turned = jnp.stack(
        [former * cosine - latter * sine_part, former * sine_part + latter * cosine], 2
    )
    return turned.reshape(row_count, HEADS * HEAD_DIM)


def conv_taps(widened, weight, batch_size, row_count, direction):
    rim_rows = (widened.shape[0] - row_count) // 2
    half_kernel = weight.shape[0] // 2
    result = jnp.zeros((row_count, widened.shape[1]), jnp.float32)
    for tap_index in range(weight.shape[0]):
        slice_start = rim_rows + direction * (tap_index - half_kernel) * batch_size
        result = (
            result
            + lax.dynamic_slice_in_dim(widened, slice_start, row_count, 0) * weight[tap_index]
        )
    return result


def tap_grads(widened, upstream, batch_size, row_count, kernel_taps):
    rim_rows = (widened.shape[0] - row_count) // 2
    half_kernel = kernel_taps // 2
    columns = []
    for tap_index in range(kernel_taps):
        slice_start = rim_rows + (tap_index - half_kernel) * batch_size
        columns.append(
            jnp.sum(lax.dynamic_slice_in_dim(widened, slice_start, row_count, 0) * upstream, 0)
        )
    return jnp.stack(columns)


def ffn_forward(inputs, gain, weight_in, weight_out):
    normed, unit_part, factor = norm_forward(inputs, gain)
    low_in = to_half(normed)
    pre_act = product(low_in, weight_in)
    activated, act_back = jax.vjp(jax.nn.silu, pre_act)
    hidden = to_half(activated)
    return (product(hidden, weight_out), (unit_part, factor, low_in, act_back, hidden))


def ffn_backward(upstream, saved, gain, weight_in, weight_out):
    unit_part, factor, low_in, act_back, hidden = saved
    grad_low = to_half(upstream)
    grad_w_out = weight_grad(hidden, grad_low)
    grad_pre = to_half(act_back(product_t(grad_low, weight_out))[0])
    grad_w_in = weight_grad(low_in, grad_pre)
    grad_in, gain_grad = norm_backward(product_t(grad_pre, weight_in), unit_part, factor, gain)
    return (grad_in, gain_grad, grad_w_in, grad_w_out)


def key_visible(source, row_ids, batch_size, shard_rows, lengths, utterance):
    key_utterance = row_ids % batch_size
    key_position = source * shard_rows + row_ids // batch_size
    key_ok = key_position < lookup(lengths, key_utterance)
    return (utterance[:, None] == key_utterance[None, :]) & key_ok[None, :]


def scaled_scores(query_heads, key_rows, score_scale):
    key_heads = key_rows.reshape(query_heads.shape)
    raw_scores = jnp.einsum(
        "qhd,khd->hqk", query_heads, key_heads, preferred_element_type=jnp.float32
    )
    return raw_scores * score_scale * LOG_BASE


def attend(running, query_heads, key_rows, value_rows, visible, score_scale):
    ceiling, weight_sum, summed = running
    scaled = scaled_scores(query_heads, key_rows, score_scale)
    lifted = jnp.maximum(ceiling, jnp.floor(jnp.max(jnp.where(visible, scaled, MASKED_SCORE), -1)))
    weights = jnp.where(
        visible, jnp.exp2(jnp.where(visible, scaled - lifted[:, :, None], -200.0)), 0.0
    )
    rescale = jnp.exp2(ceiling - lifted)
    value_heads = value_rows.reshape(query_heads.shape)
    summed = summed * rescale.T[:, :, None] + jnp.einsum(
        "hqk,khd->qhd", to_half(weights), value_heads, preferred_element_type=jnp.float32
    )
    return (lifted, weight_sum * rescale + jnp.sum(weights, -1), summed)


def attend_back(query_heads, key_rows, value_rows, visible, score_scale, ceiling, grad_av, offset):
    row_count = key_rows.shape[0]
    scaled = scaled_scores(query_heads, key_rows, score_scale)
    weights = jnp.where(
        visible, jnp.exp2(jnp.where(visible, scaled - ceiling[:, :, None], -200.0)), 0.0
    )
    key_heads = key_rows.reshape(query_heads.shape)
    value_heads = value_rows.reshape(query_heads.shape)
    grad_prob = jnp.einsum("qhd,khd->hqk", grad_av, value_heads, preferred_element_type=jnp.float32)
    grad_score = to_half(weights * (grad_prob - offset[:, :, None]) * score_scale)
    grad_query = jnp.einsum(
        "hqk,khd->qhd", grad_score, key_heads, preferred_element_type=jnp.float32
    )
    grad_key = jnp.einsum(
        "hqk,qhd->khd", grad_score, query_heads, preferred_element_type=jnp.float32
    )
    grad_value = jnp.einsum(
        "hqk,qhd->khd", to_half(weights), grad_av, preferred_element_type=jnp.float32
    )
    return (
        grad_query,
        jnp.concatenate([grad_key.reshape(row_count, -1), grad_value.reshape(row_count, -1)], 1),
    )


def local(
    features,
    d_out,
    bucket_batch,
    valid_len,
    time_start,
    time_width,
    freq_start,
    freq_width,
    gains,
    inner_gain,
    ffn1_in,
    ffn1_out,
    qkv_w,
    out_w,
    cg_up,
    cg_conv,
    cg_down,
    merge_conv,
    merge_w,
    ffn2_in,
    ffn2_out,
):
    row_count, model_width = features.shape
    half_cg = cg_down.shape[0]
    kernel_taps = cg_conv.shape[0]
    rim_rows = kernel_taps // 2 * BMAX
    score_scale = HEAD_DIM ** (-0.5)
    blk_count = lax.axis_size("blk")
    my_index = lax.axis_index("blk")
    batch_size = bucket_batch[0]
    shard_rows = row_count // batch_size
    lengths = valid_len[0]
    row_ids = jnp.arange(row_count, dtype=jnp.int32)
    utterance = row_ids % batch_size
    position = my_index * shard_rows + row_ids // batch_size
    time_low = lookup(time_start[0], utterance)
    time_high = time_low + lookup(time_width[0], utterance)
    band_low = lookup(freq_start[0], utterance)
    band_high = band_low + lookup(freq_width[0], utterance)
    frame_keep = (position < lookup(lengths, utterance)) & jnp.logical_not(
        (position >= time_low) & (position < time_high)
    )
    channel = jnp.arange(model_width, dtype=jnp.int32)
    band_hit = (channel[None, :] >= band_low[:, None]) & (channel[None, :] < band_high[:, None])
    keep_mask = (frame_keep[:, None] & jnp.logical_not(band_hit)).astype(jnp.float32)
    x_zero = features.astype(jnp.float32) * keep_mask
    cg_taps = cg_conv.astype(jnp.float32)
    merge_taps = merge_conv.astype(jnp.float32)
    first_ffn, first_saved = ffn_forward(x_zero, gains[0], ffn1_in, ffn1_out)
    x_one = x_zero + 0.5 * first_ffn
    att_normed, att_unit, att_factor = norm_forward(x_one, gains[1])
    att_low = to_half(att_normed)
    qkv_rows = product(att_low, qkv_w)
    query_heads = to_half(rotate(qkv_rows[:, :model_width], position, 1.0)).reshape(
        row_count, HEADS, HEAD_DIM
    )
    key_rows = to_half(rotate(qkv_rows[:, model_width : 2 * model_width], position, 1.0))
    value_rows = to_half(qkv_rows[:, 2 * model_width :])
    start_state = (
        jnp.full((HEADS, row_count), MASKED_SCORE, jnp.float32),
        jnp.zeros((HEADS, row_count), jnp.float32),
        jnp.zeros((row_count, HEADS, HEAD_DIM), jnp.float32),
    )

    def visible_for(source):
        return key_visible(source, row_ids, batch_size, shard_rows, lengths, utterance)

    def travel(turn_index, loop_carry):
        moving_keys, moving_values, running = loop_carry
        moving_keys, moving_values = shifted((moving_keys, moving_values), "blk", 1)
        source = (my_index - turn_index) % blk_count
        return (
            moving_keys,
            moving_values,
            attend(
                running, query_heads, moving_keys, moving_values, visible_for(source), score_scale
            ),
        )

    running = attend(
        start_state, query_heads, key_rows, value_rows, visible_for(my_index), score_scale
    )
    running = lax.fori_loop(1, blk_count, travel, (key_rows, value_rows, running))[2]
    ceiling, weight_sum, summed = running
    attended = summed / weight_sum.T[:, :, None]
    attended_low = to_half(attended.reshape(row_count, model_width))
    att_branch = product(attended_low, out_w)
    cg_normed, cg_unit, cg_factor = norm_forward(x_one, gains[2])
    cg_low = to_half(cg_normed)
    cg_pre = product(cg_low, cg_up)
    opened, gelu_back = jax.vjp(jax.nn.gelu, cg_pre)
    rest_part = opened[:, :half_cg]
    gate_normed, gate_unit, gate_factor = norm_forward(opened[:, half_cg:], inner_gain)
    gate_low = to_half(gate_normed)
    gate_wide = padded(gate_low, (("blk", 0),), rim_rows).astype(jnp.float32)
    mixed_gate = conv_taps(gate_wide, cg_taps, batch_size, row_count, 1)
    gated_low = to_half(rest_part * mixed_gate)
    cg_branch = product(gated_low, cg_down)
    joined = to_half(jnp.concatenate([att_branch, cg_branch], 1))
    joined_wide = padded(joined, (("blk", 0),), rim_rows).astype(jnp.float32)
    united_low = to_half(
        joined.astype(jnp.float32) + conv_taps(joined_wide, merge_taps, batch_size, row_count, 1)
    )
    x_two = x_one + product(united_low, merge_w)
    second_ffn, second_saved = ffn_forward(x_two, gains[3], ffn2_in, ffn2_out)
    x_three = x_two + 0.5 * second_ffn
    final_normed, final_unit, final_factor = norm_forward(x_three, gains[4])
    result = to_half(final_normed)
    grad_three, grad_final_gain = norm_backward(d_out, final_unit, final_factor, gains[4])
    back_two, grad_second_gain, grad_second_in, grad_second_out = ffn_backward(
        0.5 * grad_three, second_saved, gains[3], ffn2_in, ffn2_out
    )
    grad_two = grad_three + back_two
    merge_grad_low = to_half(grad_two)
    grad_merge_weight = weight_grad(united_low, merge_grad_low)
    grad_united = product_t(merge_grad_low, merge_w)
    conv_grad_low = to_half(grad_united)
    conv_grad_wide = padded(conv_grad_low, (("blk", 0),), rim_rows).astype(jnp.float32)
    grad_joined = grad_united + conv_taps(conv_grad_wide, merge_taps, batch_size, row_count, -1)
    grad_merge_taps = tap_grads(
        joined_wide, conv_grad_low.astype(jnp.float32), batch_size, row_count, kernel_taps
    )
    grad_att_low = to_half(grad_joined[:, :model_width])
    grad_cg_low = to_half(grad_joined[:, model_width:])
    grad_down = weight_grad(gated_low, grad_cg_low)
    grad_gated = product_t(grad_cg_low, cg_down)
    mixed_grad_low = to_half(grad_gated * rest_part)
    mixed_grad_wide = padded(mixed_grad_low, (("blk", 0),), rim_rows).astype(jnp.float32)
    grad_gate_taps = tap_grads(
        gate_wide, mixed_grad_low.astype(jnp.float32), batch_size, row_count, kernel_taps
    )
    grad_gate_in, grad_inner = norm_backward(
        conv_taps(mixed_grad_wide, cg_taps, batch_size, row_count, -1),
        gate_unit,
        gate_factor,
        inner_gain,
    )
    grad_pre_cg = to_half(gelu_back(jnp.concatenate([grad_gated * mixed_gate, grad_gate_in], 1))[0])
    grad_up = weight_grad(cg_low, grad_pre_cg)
    back_cg, grad_cg_gain = norm_backward(
        product_t(grad_pre_cg, cg_up), cg_unit, cg_factor, gains[2]
    )
    grad_out_proj = weight_grad(attended_low, grad_att_low)
    grad_attended = product_t(grad_att_low, out_w).reshape(row_count, HEADS, HEAD_DIM)
    grad_av = to_half(grad_attended / weight_sum.T[:, :, None])
    offset = jnp.sum(grad_attended * attended, -1).T / weight_sum
    zero_query = jnp.zeros((row_count, HEADS, HEAD_DIM), jnp.float32)

    def block_grads(some_keys, some_values, source):
        return attend_back(
            query_heads,
            some_keys,
            some_values,
            visible_for(source),
            score_scale,
            ceiling,
            grad_av,
            offset,
        )

    def pass_grads(pair_grads):
        return shifted(pair_grads.astype(jnp.bfloat16), "blk", 1).astype(pair_grads.dtype)

    def circle(turn_index, loop_carry):
        moving_keys, moving_values, pair_grads, grad_query = loop_carry
        source = (my_index - turn_index) % blk_count
        query_part, pair_part = block_grads(moving_keys, moving_values, source)
        moving_keys, moving_values = shifted((moving_keys, moving_values), "blk", 1)
        return (
            moving_keys,
            moving_values,
            pass_grads(pair_grads + pair_part),
            grad_query + query_part,
        )

    moving_keys, moving_values, pair_grads, grad_query = lax.fori_loop(
        0,
        blk_count - 1,
        circle,
        (key_rows, value_rows, jnp.zeros((row_count, 2 * model_width), jnp.float32), zero_query),
    )
    query_part, pair_part = block_grads(moving_keys, moving_values, (my_index + 1) % blk_count)
    grad_query = grad_query + query_part
    grad_kv = pass_grads(pair_grads + pair_part)
    grad_q = rotate(grad_query.reshape(row_count, model_width), position, -1.0)
    grad_k = rotate(grad_kv[:, :model_width], position, -1.0)
    grad_qkv_low = to_half(jnp.concatenate([grad_q, grad_k, grad_kv[:, model_width:]], 1))
    grad_qkv_proj = weight_grad(att_low, grad_qkv_low)
    back_att, grad_att_gain = norm_backward(
        product_t(grad_qkv_low, qkv_w), att_unit, att_factor, gains[1]
    )
    grad_one = grad_two + back_att + back_cg
    back_one, grad_first_gain, grad_first_in, grad_first_out = ffn_backward(
        0.5 * grad_one, first_saved, gains[0], ffn1_in, ffn1_out
    )
    grad_input = (grad_one + back_one) * keep_mask
    (
        sum_gains,
        sum_inner,
        sum_first_in,
        sum_first_out,
        sum_qkv,
        sum_out_proj,
        sum_up,
        sum_gate_taps,
        sum_down,
        sum_merge_taps,
        sum_merge_weight,
        sum_second_in,
        sum_second_out,
    ) = lax.psum(
        (
            jnp.stack(
                [grad_first_gain, grad_att_gain, grad_cg_gain, grad_second_gain, grad_final_gain]
            ),
            grad_inner,
            grad_first_in,
            grad_first_out,
            grad_qkv_proj,
            grad_out_proj,
            grad_up,
            grad_gate_taps,
            grad_down,
            grad_merge_taps,
            grad_merge_weight,
            grad_second_in,
            grad_second_out,
        ),
        ("grp", "blk"),
    )
    return (
        result,
        grad_input,
        sum_gains,
        sum_inner,
        sum_first_in,
        sum_first_out,
        sum_qkv,
        sum_out_proj,
        sum_up,
        sum_gate_taps,
        sum_down,
        sum_merge_taps,
        sum_merge_weight,
        sum_second_in,
        sum_second_out,
    )


def solution(mesh):
    in_specs = (
        P(("grp", "blk"), None),
        P(("grp", "blk"), None),
        P("grp"),
        P("grp", None),
        P("grp", None),
        P("grp", None),
        P("grp", None),
        P("grp", None),
        P(),
        P(),
        P(),
        P(),
        P(),
        P(),
        P(),
        P(),
        P(),
        P(),
        P(),
        P(),
        P(),
    )
    out_specs = (
        P(("grp", "blk"), None),
        P(("grp", "blk"), None),
        P(),
        P(),
        P(),
        P(),
        P(),
        P(),
        P(),
        P(),
        P(),
        P(),
        P(),
        P(),
        P(),
    )
    return jax.shard_map(local, mesh=mesh, in_specs=in_specs, out_specs=out_specs, check_vma=False)
```

profile of v0, /device:TPU:0, one launch (start us, length us, event | category | flops | bytes accessed | tf_op | source)
XLA Modules:
  0.0 634.6 jit_solution(10916270801041748808)
XLA Ops:
  10.7 1.5 fusion.251
  12.2 3.3 multiply_convert_fusion.3
  16.5 2.2 multiply_multiply_fusion.2
  20.2 3.0 collective-permute-start.5
  32.3 1.7 copy.110
  34.7 3.7 fusion.84
  38.4 34.1 %while.51 = (s32[]{:T(128)}, bf16[512,256]{0,1:T(8,128)(2,1)S(1)}, bf16[512,256]{0,1:T(8,128)(2,1)}, f32[4,512]{1,0:T(4,128)S(1)}, f32[4,512]{1,0:T(4,128)S(1)},...) while((s32[]{:T(128)}, bf16[512,256]{0,1:T(8,128)(2,1)S(1)}, ...), condition=%wide.region_15.16_spmd.clone.clone.clone, body=%wide.region_11.15_spmd.clone.clone.clone.sunk | while | flops 284974080 | bytes 18755988 | solution.py:280
  38.5 2.7 collective-permute-start
  41.2 1.7 collective-permute-start.1
  44.2 1.6 collective-permute-done
  48.7 1.5 fusion.351
  51.4 2.4 collective-permute-start.1
  55.1 1.6 collective-permute-done
  59.5 1.5 fusion.351
  62.2 2.4 collective-permute-start.1
  65.9 1.6 collective-permute-done
  76.5 10.0 %multiply_convert_fusion.5 = (bf16[512,512]{1,0:T(8,128)(2,1)S(1)}, f32[512,512]{1,0:T(8,128)}) fusion(f32[512,1024]{1,0:T(8,128)} %copy-done.4, f32[512]{0:T(512)} %bitcast.492, f32[572,512]{1,0:T(8,128)S(1)} %maximum_convert_fusion.2, s32[]{:T(128)S(6)} %select_n.559, f32[512]{0:T(512)} %bitcast.490, s32[]{:T(128)S(6)} %select_n.558, f32[512]{0:T(512)} %bitcast.488, ...), kind=kLoop, calls=%fused_computation.282 | loop fusion | flops 16515072 | bytes 35190904 | tf_op jit(solution)/shard_map/convert_element_type | solution.py:43
  88.3 3.1 collective-permute-start.7
  93.3 2.0 copy.88
  97.9 13.6 %add_convert_fusion = bf16[512,512]{0,1:T(8,128)(2,1)S(1)} fusion(f32[572,512]{0,1:T(8,128)S(1)} %maximum_convert_fusion, s32[]{:T(128)S(6)} %select_n.559, s32[]{:T(128)S(6)} %select_n.558, s32[]{:T(128)S(6)} %select_n.557, s32[]{:T(128)S(6)} %select_n.556, s32[]{:T(128)S(6)} %select_n.555, s32[]{:T(128)S(6)} %select_n.554, s32[]{:T(128)S(6)} %select_n.553, ...), kind=kLoop, calls=%fused_computation.281 | loop fusion | flops 17563648 | bytes 33618040 | tf_op jit(solution)/shard_map/convert_element_type | solution.py:43
  117.2 1.5 fusion.237
  119.8 1.5 fusion.208
  121.5 7.7 %fusion.148 = (f32[512]{0:T(512)}, f32[512]{0:T(512)}, f32[512]{0:T(512)}, f32[512]{0:T(512)}, f32[512]{0:T(512)}, /*index=5*/f32[512]{0:T(512)}, f32[512]{0:T(5...) fusion(f32[572,512]{0,1:T(8,128)S(1)} %maximum_convert_fusion, ...), kind=kOutput, calls=%fused_computation.239 | convolution fusion | flops 143777280 | bytes 20219968 | tf_op jit(solution)/shard_map/dot_general | solution.py:51
  130.0 6.6 %fusion.147 = (f32[512]{0:T(512)}, f32[512]{0:T(512)}, f32[512]{0:T(512)}, f32[512]{0:T(512)}, f32[512]{0:T(512)}, /*index=5*/f32[512]{0:T(512)}, f32[512]{0:T(5...) fusion(bf16[512,512]{0,1:T(8,128)(2,1)S(1)} %get-tuple-element., ...), kind=kLoop, calls=%fused_computation.238 | loop fusion | flops 7595008 | bytes 15233080 | tf_op jit(solution)/shard_map/reduce_sum | solution.py:118
  137.9 6.1 collective-permute-start.9
  145.2 5.3 stack.306
  152.0 14.0 %fusion.183 = bf16[512,512]{0,1:T(8,128)(2,1)S(1)} fusion(f32[512,512]{0,1:T(8,128)S(1)} %copy-done.30, f32[572,512]{0,1:T(8,128)S(1)} %maximum_convert_fusion.1, s32[]{:T(128)S(6)} %select_n.530, s32[]{:T(128)S(6)} %select_n.531, s32[]{:T(128)S(6)} %select_n.532, s32[]{:T(128)S(6)} %select_n.533, s32[]{:T(128)S(6)} %select_n.534, s32[]{:T(128)S(6)} %select_n.535, ...), kind=kLoop, calls=%fused_computation.286 | loop fusion | flops 16515072 | bytes 34142328 | tf_op jit(solution)/shard_map/convert.11
  166.1 5.9 fusion.117
  174.0 2.9 fusion.116
  176.9 3.6 collective-permute-start.12
  183.3 78.8 %while.52 = (s32[]{:T(128)}, bf16[512,256]{0,1:T(8,128)(2,1)S(1)}, bf16[512,256]{0,1:T(8,128)(2,1)}, f32[512,512]{0,1:T(8,128)}, f32[512,4,64]{0,2,1:T(8,128)}, ...) while((s32[]{:T(128)}, bf16[512,256]{0,1:T(8,128)(2,1)S(1)}, ...), condition=%wide.region_29.30_spmd.clone.clone.clone.clone, body=%wide.region_27.29_spmd.clone.clone.clone.clone.sunk | while | flops 688925696 | bytes 37294604 | solution.py:373
  184.8 1.7 copy.133
  187.3 2.5 fusion.365
  189.8 3.1 multiply_convert_fusion.28
  197.6 1.6 fusion.368
  199.1 4.9 collective-permute-done.4
  204.1 2.1 convert_element_type.535
  206.8 2.9 collective-permute-done.3
  211.0 1.7 copy.133
  213.4 2.5 fusion.365
  215.9 3.1 multiply_convert_fusion.28
  221.4 2.4 collective-permute-start.2
  223.8 2.6 fusion.368
  226.4 3.9 collective-permute-done.4
  230.3 2.1 convert_element_type.535
  233.0 2.9 collective-permute-done.3
  237.2 1.7 copy.133
  239.6 2.5 fusion.365
  242.1 3.1 multiply_convert_fusion.28
  247.5 2.4 collective-permute-start.2
  250.0 2.6 fusion.368
  252.5 3.9 collective-permute-done.4
  256.5 2.1 convert_element_type.535
  259.2 2.9 collective-permute-done.3
  263.0 2.6 fusion.72
  265.6 2.9 multiply_convert_fusion.1
  274.6 5.3 stack.274
  280.5 12.9 %multiply_reduce_fusion = (f32[512]{0:T(512)}, f32[512]{0:T(512)S(1)}, f32[512]{0:T(512)S(1)}, f32[512,512]{1,0:T(8,128)S(1)}) fusion(f32[512]{0:T(512)S(1)} %copy-done.72, f32[512]{0:T(512)S(1)} %copy-done.66, f32[512,1024]{1,0:T(8,128)S(1)} %copy-done.6, f32[512]{0:T(512)S(1)} %copy-done.169, f32[512]{0:T(512)S(1)} %bitcast.493, ...), kind=kLoop, calls=%fused_computation.277 | loop fusion | flops 18086400 | bytes 34678904 | tf_op jit(solution)/shard_map/reduce_sum | solution.py:70
  296.8 1.5 fusion.235
  302.3 1.5 fusion.209
  304.9 1.6 fusion.232
  312.4 119.7 %all-reduce.5.cloned.1.call-done = (f32[5,256]{1,0:T(8,128)}, f32[512]{0:T(512)}, f32[31,512]{1,0:T(8,128)}, f32[31,512]{1,0:T(8,128)}) async-done(((f32[5,256]{1,0:T(8,128)}, f32[512]{0:T(512)}, f32[31,512]{1,0:T(8,128)}, f32[31,512]{1,0:T(8,128)}), (f32[5,256]{1,0:T(8,128)}, f32[512]{0:T(512)}, f32[31,512]{1,0:T(8,128)}, f32[31,512]{1,0:T(8,128)})) %all-reduce.5.cloned.1.call-update) | async-done | bytes 134160 | tf_op jit(solution)/shard_map/psum | solution.py:408
  432.1 181.9 %all-reduce.7.cloned.1.call-done = (f32[256,1024]{1,0:T(8,128)}, f32[1024,256]{1,0:T(8,128)}, f32[256,768]{1,0:T(8,128)}, f32[256,256]{1,0:T(8,128)}, f32[256,10...) async-done(((f32[256,1024]{1,0:T(8,128)}, f32[1024,256]{1,0:T(8,128)}, f32[256,768]{1,0:T(8,128)}, ...) | async-done | bytes 7340048 | tf_op jit(solution)/shard_map/psum | solution.py:408
  616.6 2.4 copy.157
  (610 shorter events, 106.0 us)
Async XLA Ops:
  7.2 9.3 %copy-start = (bf16[256,1024]{1,0:T(8,128)(2,1)S(1)}, bf16[256,1024]{1,0:T(8,128)(2,1)}, u32[]{:S(2)}) copy-start(bf16[256,1024]{1,0:T(8,128)(2,1)} %param.39) | copy-start | bytes 1572868
  7.2 424.9 %all-reduce.5.cloned.1.call-start = ((), (), s32[]{:S(2)}) async-start(), calls=%async_computation | async-start | bytes 282624 | tf_op jit(solution)/shard_map/psum | solution.py:408
  12.2 12.2 %copy-start.170 = (f32[1,256]{1,0:T(1,128)}, f32[1,256]{1,0:T(1,128)S(1)}, u32[]{:S(2)}) copy-start(f32[1,256]{1,0:T(1,128)S(1)} %get-tuple-element.1447) | copy-start | bytes 3076
  16.1 95.4 %copy-start.8 = (f32[512,256]{0,1:T(8,128)}, f32[512,256]{0,1:T(8,128)S(1)}, u32[]{:S(2)}) copy-start(f32[512,256]{0,1:T(8,128)S(1)} %get-tuple-element.1461) | copy-start | bytes 1572868
  16.1 8.3 %copy-start.61 = (f32[512]{0:T(512)}, f32[512]{0:T(512)S(1)}, u32[]{:S(2)}) copy-start(f32[512]{0:T(512)S(1)} %broadcast_multiply_fusion.16) | copy-start | bytes 6148
  16.2 8.2 %copy-start.69 = (f32[512]{0:T(512)}, f32[512]{0:T(512)S(1)}, u32[]{:S(2)}) copy-start(f32[512]{0:T(512)S(1)} %add_rsqrt_fusion.3) | copy-start | bytes 6148
  20.2 55.3 %collective-permute-start.5 = (bf16[30,512]{1,0:T(8,128)(2,1)}, bf16[30,512]{1,0:T(8,128)(2,1)}, u32[]{:S(2)}, u32[]{:S(2)}) collective-permute-start(bf16[30,512]{1,0:T(8,128)(2,1)} %get-tuple-element.1377), channel_id=1, source_target_pairs={{0,1},{1,2},{2,3},{4,5},{5,6},{6,7},{8,9},{9,10},{10,11},{12,13},{... | collective-permute-start | bytes 92168 | tf_op jit(solution)/shard_map/ppermute | solution.py:31
  23.1 52.4 %collective-permute-start.6 = (bf16[30,512]{1,0:T(8,128)(2,1)}, bf16[30,512]{1,0:T(8,128)(2,1)}, u32[]{:S(2)}, u32[]{:S(2)}) collective-permute-start(bf16[30,512]{1,0:T(8,128)(2,1)} %get-tuple-element.1378), channel_id=1, source_target_pairs={{1,0},{2,1},{3,2},{5,4},{6,5},{7,6},{9,8},{10,9},{11,10},{13,12},{... | collective-permute-start | bytes 92168 | tf_op jit(solution)/shard_map/ppermute | solution.py:32
  38.4 36.2 %copy-start.54 = (bf16[31,512]{1,0:T(8,128)(2,1)S(1)}, bf16[31,512]{1,0:T(8,128)(2,1)}, u32[]{:S(2)}) copy-start(bf16[31,512]{1,0:T(8,128)(2,1)} %param.40) | copy-start | bytes 95236
  38.5 7.3 %collective-permute-start = (bf16[512,256]{0,1:T(8,128)(2,1)S(1)}, bf16[512,256]{0,1:T(8,128)(2,1)S(1)}, u32[]{:S(2)}, u32[]{:S(2)}) collective-permute-start(bf16[512,256]{0,1:T(8,128)(2,1)S(1)} %get-tuple-element.1688), channel_id=1, source_target_pairs={{3,0},{0,1},{1,2},{2,3},{7,4},{4,5},{5,6},{6,7},{11,8},{8,9},{9,10... | collective-permute-start | bytes 786440 | tf_op jit(solution)/shard_map/while/body/eval_jaxpr/ppermute | solution.py:21
  41.2 7.4 %collective-permute-start.1 = (bf16[512,256]{0,1:T(8,128)(2,1)}, bf16[512,256]{0,1:T(8,128)(2,1)S(1)}, u32[]{:S(2)}, u32[]{:S(2)}) collective-permute-start(bf16[512,256]{0,1:T(8,128)(2,1)} %get-tuple-element.1689), channel_id=1, source_target_pairs={{3,0},{0,1},{1,2},{2,3},{7,4},{4,5},{5,6},{6,7},{11,8},{8,9},{9,10... | collective-permute-start | bytes 786440 | tf_op jit(solution)/shard_map/while/body/eval_jaxpr/ppermute | solution.py:21
  50.9 5.8 collective-permute-start
  51.4 8.1 %collective-permute-start.1 = (bf16[512,256]{0,1:T(8,128)(2,1)}, bf16[512,256]{0,1:T(8,128)(2,1)S(1)}, u32[]{:S(2)}, u32[]{:S(2)}) collective-permute-start(bf16[512,256]{0,1:T(8,128)(2,1)} %get-tuple-element.1689), channel_id=1, source_target_pairs={{3,0},{0,1},{1,2},{2,3},{7,4},{4,5},{5,6},{6,7},{11,8},{8,9},{9,10... | collective-permute-start | bytes 786440 | tf_op jit(solution)/shard_map/while/body/eval_jaxpr/ppermute | solution.py:21
  61.7 5.8 collective-permute-start
  62.2 8.1 %collective-permute-start.1 = (bf16[512,256]{0,1:T(8,128)(2,1)}, bf16[512,256]{0,1:T(8,128)(2,1)S(1)}, u32[]{:S(2)}, u32[]{:S(2)}) collective-permute-start(bf16[512,256]{0,1:T(8,128)(2,1)} %get-tuple-element.1689), channel_id=1, source_target_pairs={{3,0},{0,1},{1,2},{2,3},{7,4},{4,5},{5,6},{6,7},{11,8},{8,9},{9,10... | collective-permute-start | bytes 786440 | tf_op jit(solution)/shard_map/while/body/eval_jaxpr/ppermute | solution.py:21
  76.4 10.0 %copy-start.50 = (bf16[512,256]{1,0:T(8,128)(2,1)S(1)}, bf16[512,256]{1,0:T(8,128)(2,1)}, u32[]{:S(2)}) copy-start(bf16[512,256]{1,0:T(8,128)(2,1)} %param.41) | copy-start | bytes 786436
  76.5 16.2 %copy-start.56 = (bf16[31,512]{1,0:T(8,128)(2,1)S(1)}, bf16[31,512]{1,0:T(8,128)(2,1)}, u32[]{:S(2)}) copy-start(bf16[31,512]{1,0:T(8,128)(2,1)} %param.42) | copy-start | bytes 95236
  88.3 7.4 %collective-permute-start.7 = (bf16[30,512]{0,1:T(8,128)(2,1)}, bf16[30,512]{0,1:T(8,128)(2,1)}, u32[]{:S(2)}, u32[]{:S(2)}) collective-permute-start(bf16[30,512]{0,1:T(8,128)(2,1)} %get-tuple-element.1375), channel_id=1, source_target_pairs={{0,1},{1,2},{2,3},{4,5},{5,6},{6,7},{8,9},{9,10},{10,11},{12,13},{... | collective-permute-start | bytes 92168 | tf_op jit(solution)/shard_map/ppermute | solution.py:31
  91.4 4.8 collective-permute-start.8
  97.9 13.6 %copy-start.49 = (bf16[512,256]{1,0:T(8,128)(2,1)S(1)}, bf16[512,256]{1,0:T(8,128)(2,1)}, u32[]{:S(2)}) copy-start(bf16[512,256]{1,0:T(8,128)(2,1)} %param.43) | copy-start | bytes 786436
  121.5 22.5 %copy-start.11 = (f32[512,256]{0,1:T(8,128)}, f32[512,256]{0,1:T(8,128)S(1)}, u32[]{:S(2)}) copy-start(f32[512,256]{0,1:T(8,128)S(1)} %multiply_add_fusion.3) | copy-start | bytes 1572868
  136.7 14.2 %collective-permute-start.10 = (bf16[30,512]{0,1:T(8,128)(2,1)}, bf16[30,512]{0,1:T(8,128)(2,1)S(1)}, u32[]{:S(2)}, u32[]{:S(2)}) collective-permute-start(bf16[30,512]{0,1:T(8,128)(2,1)} %get-tuple-element.1374), channel_id=1, source_target_pairs={{1,0},{2,1},{3,2},{5,4},{6,5},{7,6},{9,8},{10,9},{11,10},{13,12},{... | collective-permute-start | bytes 92168 | tf_op jit(solution)/shard_map/ppermute | solution.py:32
  137.9 12.9 %collective-permute-start.9 = (bf16[30,512]{0,1:T(8,128)(2,1)}, bf16[30,512]{0,1:T(8,128)(2,1)S(1)}, u32[]{:S(2)}, u32[]{:S(2)}) collective-permute-start(bf16[30,512]{0,1:T(8,128)(2,1)} %get-tuple-element.1373), channel_id=1, source_target_pairs={{0,1},{1,2},{2,3},{4,5},{5,6},{6,7},{8,9},{9,10},{10,11},{12,13},{... | collective-permute-start | bytes 92168 | tf_op jit(solution)/shard_map/ppermute | solution.py:31
  152.0 14.0 %copy-start.5 = (f32[512,1024]{1,0:T(8,128)S(1)}, f32[512,1024]{1,0:T(8,128)}, u32[]{:S(2)}) copy-start(f32[512,1024]{1,0:T(8,128)} %copy-done.4) | copy-start | bytes 6291460
  152.0 14.0 %copy-start.51 = (bf16[512,256]{1,0:T(8,128)(2,1)S(1)}, bf16[512,256]{1,0:T(8,128)(2,1)}, u32[]{:S(2)}) copy-start(bf16[512,256]{1,0:T(8,128)(2,1)} %param.41) | copy-start | bytes 786436
  174.0 7.8 %copy-start.28 = (f32[512,4,64]{0,2,1:T(8,128)S(1)}, f32[512,4,64]{0,2,1:T(8,128)}, u32[]{:S(2)}) copy-start(f32[512,4,64]{0,2,1:T(8,128)} %copy-done.27) | copy-start | bytes 1572868
  174.0 9.3 %copy-start.60 = (s32[1,2]{1,0:T(1,128)S(1)}, s32[1,2]{1,0:T(1,128)}, u32[]{:S(2)}) copy-start(s32[1,2]{1,0:T(1,128)} %param.28) | copy-start | bytes 28
  176.9 103.1 %collective-permute-start.12 = (bf16[30,512]{1,0:T(8,128)(2,1)}, bf16[30,512]{1,0:T(8,128)(2,1)S(1)}, u32[]{:S(2)}, u32[]{:S(2)}) collective-permute-start(bf16[30,512]{1,0:T(8,128)(2,1)} %get-tuple-element.1371), channel_id=1, source_target_pairs={{0,1},{1,2},{2,3},{4,5},{5,6},{6,7},{8,9},{9,10},{10,11},{12,13},{... | collective-permute-start | bytes 92168 | tf_op jit(solution)/shard_map/ppermute | solution.py:31
  180.5 99.4 %collective-permute-start.13 = (bf16[30,512]{1,0:T(8,128)(2,1)S(1)}, bf16[30,512]{1,0:T(8,128)(2,1)S(1)}, u32[]{:S(2)}, u32[]{:S(2)}) collective-permute-start(bf16[30,512]{1,0:T(8,128)(2,1)S(1)} %get-tuple-element.1372), channel_id=1, source_target_pairs={{1,0},{2,1},{3,2},{5,4},{6,5},{7,6},{9,8},{10,9},{11,10},{13,12},{... | collective-permute-start | bytes 92168 | tf_op jit(solution)/shard_map/ppermute | solution.py:32
  195.2 8.9 %collective-permute-start.4 = (bf16[512,512]{0,1:T(8,128)(2,1)}, bf16[512,512]{0,1:T(8,128)(2,1)}, u32[]{:S(2)}, u32[]{:S(2)}) collective-permute-start(bf16[512,512]{0,1:T(8,128)(2,1)} %fusion.367), channel_id=1, source_target_pairs={{3,0},{0,1},{1,2},{2,3},{7,4},{4,5},{5,6},{6,7},{11,8},{8,9},{9,10... | collective-permute-start | bytes 1572872 | tf_op jit(solution)/shard_map/while/body/eval_jaxpr/ppermute | solution.py:21
  196.3 10.5 %collective-permute-start.2 = (bf16[512,256]{0,1:T(8,128)(2,1)S(1)}, bf16[512,256]{0,1:T(8,128)(2,1)S(1)}, u32[]{:S(2)}, u32[]{:S(2)}) collective-permute-start(bf16[512,256]{0,1:T(8,128)(2,1)S(1)} %copy.132), channel_id=1, source_target_pairs={{3,0},{0,1},{1,2},{2,3},{7,4},{4,5},{5,6},{6,7},{11,8},{8,9},{9,10... | collective-permute-start | bytes 786440 | tf_op jit(solution)/shard_map/while/body/eval_jaxpr/ppermute | solution.py:21
  197.6 12.2 %collective-permute-start.3 = (bf16[512,256]{0,1:T(8,128)(2,1)}, bf16[512,256]{0,1:T(8,128)(2,1)}, u32[]{:S(2)}, u32[]{:S(2)}) collective-permute-start(bf16[512,256]{0,1:T(8,128)(2,1)} %copy.133), channel_id=1, source_target_pairs={{3,0},{0,1},{1,2},{2,3},{7,4},{4,5},{5,6},{6,7},{11,8},{8,9},{9,10... | collective-permute-start | bytes 786440 | tf_op jit(solution)/shard_map/while/body/eval_jaxpr/ppermute | solution.py:21
  221.4 8.9 %collective-permute-start.4 = (bf16[512,512]{0,1:T(8,128)(2,1)}, bf16[512,512]{0,1:T(8,128)(2,1)}, u32[]{:S(2)}, u32[]{:S(2)}) collective-permute-start(bf16[512,512]{0,1:T(8,128)(2,1)} %fusion.367), channel_id=1, source_target_pairs={{3,0},{0,1},{1,2},{2,3},{7,4},{4,5},{5,6},{6,7},{11,8},{8,9},{9,10... | collective-permute-start | bytes 1572872 | tf_op jit(solution)/shard_map/while/body/eval_jaxpr/ppermute | solution.py:21
  221.4 11.6 %collective-permute-start.2 = (bf16[512,256]{0,1:T(8,128)(2,1)S(1)}, bf16[512,256]{0,1:T(8,128)(2,1)S(1)}, u32[]{:S(2)}, u32[]{:S(2)}) collective-permute-start(bf16[512,256]{0,1:T(8,128)(2,1)S(1)} %copy.132), channel_id=1, source_target_pairs={{3,0},{0,1},{1,2},{2,3},{7,4},{4,5},{5,6},{6,7},{11,8},{8,9},{9,10... | collective-permute-start | bytes 786440 | tf_op jit(solution)/shard_map/while/body/eval_jaxpr/ppermute | solution.py:21
  223.7 12.2 %collective-permute-start.3 = (bf16[512,256]{0,1:T(8,128)(2,1)}, bf16[512,256]{0,1:T(8,128)(2,1)}, u32[]{:S(2)}, u32[]{:S(2)}) collective-permute-start(bf16[512,256]{0,1:T(8,128)(2,1)} %copy.133), channel_id=1, source_target_pairs={{3,0},{0,1},{1,2},{2,3},{7,4},{4,5},{5,6},{6,7},{11,8},{8,9},{9,10... | collective-permute-start | bytes 786440 | tf_op jit(solution)/shard_map/while/body/eval_jaxpr/ppermute | solution.py:21
  247.5 8.9 %collective-permute-start.4 = (bf16[512,512]{0,1:T(8,128)(2,1)}, bf16[512,512]{0,1:T(8,128)(2,1)}, u32[]{:S(2)}, u32[]{:S(2)}) collective-permute-start(bf16[512,512]{0,1:T(8,128)(2,1)} %fusion.367), channel_id=1, source_target_pairs={{3,0},{0,1},{1,2},{2,3},{7,4},{4,5},{5,6},{6,7},{11,8},{8,9},{9,10... | collective-permute-start | bytes 1572872 | tf_op jit(solution)/shard_map/while/body/eval_jaxpr/ppermute | solution.py:21
  247.5 11.6 %collective-permute-start.2 = (bf16[512,256]{0,1:T(8,128)(2,1)S(1)}, bf16[512,256]{0,1:T(8,128)(2,1)S(1)}, u32[]{:S(2)}, u32[]{:S(2)}) collective-permute-start(bf16[512,256]{0,1:T(8,128)(2,1)S(1)} %copy.132), channel_id=1, source_target_pairs={{3,0},{0,1},{1,2},{2,3},{7,4},{4,5},{5,6},{6,7},{11,8},{8,9},{9,10... | collective-permute-start | bytes 786440 | tf_op jit(solution)/shard_map/while/body/eval_jaxpr/ppermute | solution.py:21
  249.9 12.2 %collective-permute-start.3 = (bf16[512,256]{0,1:T(8,128)(2,1)}, bf16[512,256]{0,1:T(8,128)(2,1)}, u32[]{:S(2)}, u32[]{:S(2)}) collective-permute-start(bf16[512,256]{0,1:T(8,128)(2,1)} %copy.133), channel_id=1, source_target_pairs={{3,0},{0,1},{1,2},{2,3},{7,4},{4,5},{5,6},{6,7},{11,8},{8,9},{9,10... | collective-permute-start | bytes 786440 | tf_op jit(solution)/shard_map/while/body/eval_jaxpr/ppermute | solution.py:21
  273.0 25.3 %collective-permute-start.11 = (bf16[512,512]{0,1:T(8,128)(2,1)}, bf16[512,512]{0,1:T(8,128)(2,1)}, u32[]{:S(2)}, u32[]{:S(2)}) collective-permute-start(bf16[512,512]{0,1:T(8,128)(2,1)} %fusion.182), channel_id=1, source_target_pairs={{3,0},{0,1},{1,2},{2,3},{7,4},{4,5},{5,6},{6,7},{11,8},{8,9},{9,10... | collective-permute-start | bytes 1572872 | tf_op jit(solution)/shard_map/ppermute | solution.py:21
  273.1 7.1 %copy-start.6 = (f32[512,1024]{1,0:T(8,128)S(1)}, f32[512,1024]{1,0:T(8,128)}, u32[]{:S(2)}) copy-start(f32[512,1024]{1,0:T(8,128)} %copy-done.4) | copy-start | bytes 6291460
  273.1 7.1 %copy-start.66 = (f32[512]{0:T(512)S(1)}, f32[512]{0:T(512)}, u32[]{:S(2)}) copy-start(f32[512]{0:T(512)} %copy-done.65) | copy-start | bytes 6148
  273.1 7.1 %copy-start.72 = (f32[512]{0:T(512)S(1)}, f32[512]{0:T(512)}, u32[]{:S(2)}) copy-start(f32[512]{0:T(512)} %copy-done.71) | copy-start | bytes 6148
  273.1 7.1 %copy-start.137 = (f32[1,512]{1,0:T(1,128)S(1)}, f32[1,512]{1,0:T(1,128)}, u32[]{:S(2)}) copy-start(f32[1,512]{1,0:T(1,128)} %get-tuple-element.1412) | copy-start | bytes 6148
  273.1 7.1 %copy-start.138 = (f32[1,512]{1,0:T(1,128)S(1)}, f32[1,512]{1,0:T(1,128)}, u32[]{:S(2)}) copy-start(f32[1,512]{1,0:T(1,128)} %get-tuple-element.1413) | copy-start | bytes 6148
  273.1 7.1 %copy-start.139 = (f32[1,512]{1,0:T(1,128)S(1)}, f32[1,512]{1,0:T(1,128)}, u32[]{:S(2)}) copy-start(f32[1,512]{1,0:T(1,128)} %get-tuple-element.1414) | copy-start | bytes 6148
  273.1 7.1 %copy-start.140 = (f32[1,512]{1,0:T(1,128)S(1)}, f32[1,512]{1,0:T(1,128)}, u32[]{:S(2)}) copy-start(f32[1,512]{1,0:T(1,128)} %get-tuple-element.1415) | copy-start | bytes 6148
  273.1 7.1 %copy-start.141 = (f32[1,512]{1,0:T(1,128)S(1)}, f32[1,512]{1,0:T(1,128)}, u32[]{:S(2)}) copy-start(f32[1,512]{1,0:T(1,128)} %get-tuple-element.1416) | copy-start | bytes 6148
  273.2 7.1 %copy-start.142 = (f32[1,512]{1,0:T(1,128)S(1)}, f32[1,512]{1,0:T(1,128)}, u32[]{:S(2)}) copy-start(f32[1,512]{1,0:T(1,128)} %get-tuple-element.1417) | copy-start | bytes 6148
  273.2 7.1 %copy-start.143 = (f32[1,512]{1,0:T(1,128)S(1)}, f32[1,512]{1,0:T(1,128)}, u32[]{:S(2)}) copy-start(f32[1,512]{1,0:T(1,128)} %get-tuple-element.1418) | copy-start | bytes 6148
  273.2 7.1 %copy-start.144 = (f32[1,512]{1,0:T(1,128)S(1)}, f32[1,512]{1,0:T(1,128)}, u32[]{:S(2)}) copy-start(f32[1,512]{1,0:T(1,128)} %get-tuple-element.1419) | copy-start | bytes 6148
  273.2 7.1 %copy-start.145 = (f32[1,512]{1,0:T(1,128)S(1)}, f32[1,512]{1,0:T(1,128)}, u32[]{:S(2)}) copy-start(f32[1,512]{1,0:T(1,128)} %get-tuple-element.1420) | copy-start | bytes 6148
  273.2 7.1 %copy-start.146 = (f32[1,512]{1,0:T(1,128)S(1)}, f32[1,512]{1,0:T(1,128)}, u32[]{:S(2)}) copy-start(f32[1,512]{1,0:T(1,128)} %get-tuple-element.1421) | copy-start | bytes 6148
  273.2 7.1 %copy-start.147 = (f32[1,512]{1,0:T(1,128)S(1)}, f32[1,512]{1,0:T(1,128)}, u32[]{:S(2)}) copy-start(f32[1,512]{1,0:T(1,128)} %get-tuple-element.1422) | copy-start | bytes 6148
  273.2 7.1 %copy-start.148 = (f32[1,512]{1,0:T(1,128)S(1)}, f32[1,512]{1,0:T(1,128)}, u32[]{:S(2)}) copy-start(f32[1,512]{1,0:T(1,128)} %get-tuple-element.1423) | copy-start | bytes 6148
  273.2 7.1 %copy-start.149 = (f32[1,512]{1,0:T(1,128)S(1)}, f32[1,512]{1,0:T(1,128)}, u32[]{:S(2)}) copy-start(f32[1,512]{1,0:T(1,128)} %get-tuple-element.1424) | copy-start | bytes 6148
  273.2 7.1 %copy-start.150 = (f32[1,512]{1,0:T(1,128)S(1)}, f32[1,512]{1,0:T(1,128)}, u32[]{:S(2)}) copy-start(f32[1,512]{1,0:T(1,128)} %get-tuple-element.1425) | copy-start | bytes 6148
  273.2 7.1 %copy-start.151 = (f32[1,512]{1,0:T(1,128)S(1)}, f32[1,512]{1,0:T(1,128)}, u32[]{:S(2)}) copy-start(f32[1,512]{1,0:T(1,128)} %get-tuple-element.1426) | copy-start | bytes 6148
  273.3 7.1 %copy-start.152 = (f32[1,512]{1,0:T(1,128)S(1)}, f32[1,512]{1,0:T(1,128)}, u32[]{:S(2)}) copy-start(f32[1,512]{1,0:T(1,128)} %get-tuple-element.1427) | copy-start | bytes 6148
  273.3 7.1 %copy-start.153 = (f32[1,512]{1,0:T(1,128)S(1)}, f32[1,512]{1,0:T(1,128)}, u32[]{:S(2)}) copy-start(f32[1,512]{1,0:T(1,128)} %get-tuple-element.1428) | copy-start | bytes 6148
  273.3 7.1 %copy-start.154 = (f32[1,512]{1,0:T(1,128)S(1)}, f32[1,512]{1,0:T(1,128)}, u32[]{:S(2)}) copy-start(f32[1,512]{1,0:T(1,128)} %get-tuple-element.1429) | copy-start | bytes 6148
  273.3 7.1 %copy-start.155 = (f32[1,512]{1,0:T(1,128)S(1)}, f32[1,512]{1,0:T(1,128)}, u32[]{:S(2)}) copy-start(f32[1,512]{1,0:T(1,128)} %get-tuple-element.1430) | copy-start | bytes 6148
  273.3 7.1 %copy-start.156 = (f32[1,512]{1,0:T(1,128)S(1)}, f32[1,512]{1,0:T(1,128)}, u32[]{:S(2)}) copy-start(f32[1,512]{1,0:T(1,128)} %get-tuple-element.1431) | copy-start | bytes 6148
  273.3 7.1 %copy-start.157 = (f32[1,512]{1,0:T(1,128)S(1)}, f32[1,512]{1,0:T(1,128)}, u32[]{:S(2)}) copy-start(f32[1,512]{1,0:T(1,128)} %get-tuple-element.1432) | copy-start | bytes 6148
  307.9 306.0 %all-reduce.7.cloned.1.call-start = ((), (), s32[]{:S(2)}) async-start(), calls=%async_computation.1 | async-start | bytes 14680064 | tf_op jit(solution)/shard_map/psum | solution.py:408
  (159 other events, 401.7 us)
Sparse Core Ops, SparseCore 0:
  308.1 123.9 all-reduce.4
  439.7 174.2 all-reduce.6
where the time goes:
time: 644 us; the launch traced here: 635 us
  waiting for transfers between devices  332 us (52%)
  other arithmetic  98.4 us (15%)
  matrix products  88 us (14%)
  local copies, waits for them, and re-layouts  58.6 us (9%)
  starting transfers between devices  38.4 us (6%)
  between operations  18.3 us (3%)
    psum x2, waiting for transfers between devices, local(): lax.psum((jnp.stack([grad_first_gain, grad_att_gain, grad_cg_gain, grad_s...  302 us
    unnamed x402, local copies, waits for them, and re-layouts  30.1 us
    ppermute x16, waiting for transfers between devices, shifted(): return lax.ppermute(block, axis, route)  29.9 us
    convert_element_type x6, other arithmetic, to_half(): return value.astype(jnp.bfloat16)  25.3 us
    dot_general x9, matrix products, product_t(): lax.dot_general(left, right, (((1,), (1,)), ((), ())), preferred_element_...  18.9 us
    ppermute x16, starting transfers between devices, shifted(): return lax.ppermute(block, axis, route)  17.5 us
    ppermute x4, starting transfers between devices, padded(): before = lax.ppermute(last, axis, up)  15.7 us
    another operation x3, other arithmetic  14.2 us
  transfers between devices with their start and end apart: 26, of which 18 were waited for; matrix products, arithmetic and copies ran while one was open for 20% of the time, Pallas kernels for 0%

commit v1 on v0

v1 whole, which is shorter than its diff:
```python
import functools
import math

import jax
import jax.numpy as jnp
import numpy as np
from jax import lax
from jax.experimental import pallas as pl
from jax.experimental.pallas import tpu as pltpu
from jax.sharding import PartitionSpec as P

HEADS = 4
HEAD_DIM = 64
HALO = 32
LOG_BASE = 1.4426950408889634
EPSILON = 1e-05
SCORE_SCALE = HEAD_DIM ** (-0.5)
EXP_SCALE = SCORE_SCALE * LOG_BASE
HIDE = -(2.0 ** 100)
AXES = ("grp", "blk")
F32 = jnp.float32
BF16 = jnp.bfloat16
LANES = 128
VMEM_BYTES = 16 * 1024 * 1024
UNIT = 0.35e9


def mm(left, right):
    return jnp.dot(left, right, preferred_element_type=F32)


def mm_nt(left, right):
    return lax.dot_general(left, right, (((1,), (1,)), ((), ())), preferred_element_type=F32)


def mm_tn(left, right):
    return lax.dot_general(left, right, (((0,), (0,)), ((), ())), preferred_element_type=F32)


def unit(v):
    center = v - jnp.mean(v, -1, keepdims=True)
    rs = lax.rsqrt(jnp.mean(center * center, -1, keepdims=True) + EPSILON)
    return center * rs, rs


def unit_back(up, m, rs, gain):
    eg = up * gain
    grad = rs * (eg - jnp.mean(eg, -1, keepdims=True) - m * jnp.mean(eg * m, -1, keepdims=True))
    return grad, jnp.sum(up * m, 0, keepdims=True)


def silu_parts(u):
    sig = 0.5 + 0.5 * jnp.tanh(0.5 * u)
    h = u * sig
    return h, sig + h * (1.0 - sig)


def gelu_parts(t):
    root = math.sqrt(2.0 / math.pi)
    t2 = t * t
    th = jnp.tanh(root * t * (1.0 + 0.044715 * t2))
    half = 0.5 + 0.5 * th
    slope = half + 0.5 * root * t * (1.0 - th * th) * (1.0 + 3.0 * 0.044715 * t2)
    return t * half, slope


def rows_of(sc, r0, shape):
    row = lax.broadcasted_iota(jnp.int32, shape, 0) + r0
    shift = sc[0] - 1
    utt = row & shift
    pos = (row >> shift) + sc[1] * (512 >> shift)
    return utt, pos


def keep_mask(sc, r0, shape):
    utt, pos = rows_of(sc, r0, shape)
    ch = lax.broadcasted_iota(jnp.int32, shape, 1)
    first = utt == 0

    def pick(i):
        return jnp.where(first, sc[i], sc[i + 1])

    ok = (pos < pick(2)) & jnp.logical_not((pos >= pick(4)) & (pos < pick(6)))
    ok = ok & jnp.logical_not((ch >= pick(8)) & (ch < pick(10)))
    return ok


def turn_tables(sc, freq, rows):
    shift = sc[0] - 1
    coarse = lax.broadcasted_iota(jnp.int32, (rows // 16, LANES), 0) * 16
    fine = lax.broadcasted_iota(jnp.int32, (16, LANES), 0)
    a = ((coarse >> shift) + sc[1] * (rows >> shift)).astype(F32) * freq
    c = (fine >> shift).astype(F32) * freq
    ca, sa, cc, cs = jnp.cos(a), jnp.sin(a), jnp.cos(c), jnp.sin(c)
    cos = ca[:, None, :] * cc[None] - sa[:, None, :] * cs[None]
    sin = sa[:, None, :] * cc[None] + ca[:, None, :] * cs[None]
    return cos.reshape(rows, LANES), sin.reshape(rows, LANES)


def rotate(v, cos, sin, direction):
    lane = lax.broadcasted_iota(jnp.int32, (v.shape[0], LANES), 1)
    lower = (lane & 63) < 32
    signed = jnp.where(lower, -direction, direction) * sin
    parts = []
    for i in range(v.shape[1] // LANES):
        p = v[:, i * LANES : (i + 1) * LANES]
        other = jnp.where(lower, pltpu.roll(p, LANES - 32, 1), pltpu.roll(p, 32, 1))
        parts.append(p * cos + other * signed)
    return jnp.concatenate(parts, 1)


def edge_sends(sc, refs, a_ref, b_ref):
    odd = (sc[1] & 1) == 1
    col = 0
    for ref in refs if isinstance(refs, tuple) else (refs,):
        rows, width = ref.shape
        first = ref[0:HALO, :]
        last = ref[rows - HALO : rows, :]
        cols = slice(col, col + width)
        col += width

        @pl.when(odd)
        def _():
            a_ref[:, cols] = first
            b_ref[:, cols] = last

        @pl.when(jnp.logical_not(odd))
        def _():
            a_ref[:, cols] = last
            b_ref[:, cols] = first


def fill_wide(sc, wide, sources, ha, hb):
    odd = (sc[1] & 1) == 1
    at = 0
    for z in sources:
        rows, width = z.shape
        for c in range(width // LANES):
            cols = slice(at * LANES, (at + 1) * LANES)
            a, b = ha[:, cols].astype(F32), hb[:, cols].astype(F32)
            wide[at, 0:HALO, :] = jnp.where(odd, a, b)
            wide[at, HALO : HALO + rows, :] = z[:, c * LANES : (c + 1) * LANES].astype(F32)
            wide[at, HALO + rows : 2 * HALO + rows, :] = jnp.where(odd, b, a)
            at += 1


CONV_ROWS = 64


def conv_fwd(sc, wide, taps, out, rows):
    batch = sc[0]
    for c in range(taps.shape[1] // LANES):
        cols = slice(c * LANES, (c + 1) * LANES)
        ws = [taps[k : k + 1, cols].astype(F32) for k in range(31)]

        def body(i, carry):
            r0 = pl.multiple_of(i * CONV_ROWS, CONV_ROWS)
            acc = jnp.zeros((CONV_ROWS, LANES), F32)
            for k in range(31):
                acc = acc + wide[c, pl.ds(r0 + HALO + batch * (k - 15), CONV_ROWS), :] * ws[k]
            out[pl.ds(r0, CONV_ROWS), cols] = acc
            return carry

        lax.fori_loop(0, rows // CONV_ROWS, body, 0)


BACK_ROWS = 32


def conv_back(sc, wide, taps, z, out, tap_out, rows):
    batch = sc[0]
    for c in range(taps.shape[1] // LANES):
        cols = slice(c * LANES, (c + 1) * LANES)
        for start, stop in ((0, 16), (16, 31)):
            ws = [taps[k : k + 1, cols].astype(F32) for k in range(start, stop)]

            def body(i, sums):
                r0 = pl.multiple_of(i * BACK_ROWS, BACK_ROWS)
                here = pl.ds(r0, BACK_ROWS)
                zc = z[here, cols].astype(F32)
                acc = out[here, cols]
                new = []
                for k in range(start, stop):
                    e = wide[c, pl.ds(r0 + HALO - batch * (k - 15), BACK_ROWS), :]
                    acc = acc + e * ws[k - start]
                    prod = (e * zc).reshape(BACK_ROWS // 8, 8, LANES)
                    new.append(sums[k - start] + jnp.sum(prod, 0))
                out[here, cols] = acc
                return tuple(new)

            zero = tuple(jnp.zeros((8, LANES), F32) for _ in range(stop - start))
            sums = lax.fori_loop(0, rows // BACK_ROWS, body, zero)
            for k in range(start, stop):
                tap_out[k : k + 1, cols] = jnp.sum(sums[k - start], 0, keepdims=True)


def tiles(rows, size=256):
    size = min(size, rows)
    return [slice(i, i + size) for i in range(0, rows, size)]


def pre_kernel(*refs):
    hbm, refs = refs[:12], refs[12:]
    sc, x1_o, a1_o, h_o, d_o, a2_o, q_o, kv_o, kvs_o = refs[:9]
    bb, vl, ts, tw, fs, fw, gains, freq, feat, w1, w2, wq, sems = refs[9:]
    loads = [
        pltpu.make_async_copy(src, dst, sems.at[i])
        for i, (src, dst) in enumerate(zip(hbm, (bb, vl, ts, tw, fs, fw, gains, freq, feat, w1, w2, wq)))
    ]
    for load in loads:
        load.start()
    for load in loads[:8]:
        load.wait()
    sc[0] = bb[0]
    sc[1] = lax.axis_index("blk")
    for i in range(2):
        sc[2 + i] = vl[0, i]
        sc[4 + i] = ts[0, i]
        sc[6 + i] = ts[0, i] + tw[0, i]
        sc[8 + i] = fs[0, i]
        sc[10 + i] = fs[0, i] + fw[0, i]
    for i in range(12, 16):
        sc[i] = 0
    loads = loads[8:]
    rows = feat.shape[0]
    cos, sin = turn_tables(sc, freq[...], rows)
    parts = tiles(rows)
    for i, t in enumerate(parts):
        shape = (t.stop - t.start, 256)
        if i == 0:
            loads[0].wait()
        x = jnp.where(keep_mask(sc, t.start, shape), feat[t, :].astype(F32), 0.0)
        m, _ = unit(x)
        a1 = (m * gains[0:1, :]).astype(BF16)
        a1_o[t, :] = a1
        if i == 0:
            loads[1].wait()
        h, d = silu_parts(mm(a1, w1[...]))
        h = h.astype(BF16)
        h_o[t, :] = h
        d_o[t, :] = d.astype(BF16)
        if i == 0:
            loads[2].wait()
        x1 = x + 0.5 * mm(h, w2[...])
        x1_o[t, :] = x1
        m, _ = unit(x1)
        a2 = (m * gains[1:2, :]).astype(BF16)
        a2_o[t, :] = a2
        if i == 0:
            loads[3].wait()
        qkv = mm(a2, wq[...])
        q_o[t, :] = rotate(qkv[:, 0:256], cos[t], sin[t], 1.0).astype(BF16)
        k = rotate(qkv[:, 256:512], cos[t], sin[t], 1.0).astype(BF16)
        v = qkv[:, 512:768].astype(BF16)
        for o in (kv_o, kvs_o):
            o[t, 0:256] = k
            o[t, 256:512] = v


def gate_kernel(sc, x1, gains, inner, up, a3_o, rest_o, slope_o, n_o, mg_o, rs_o, ea_o, eb_o):
    rows = x1.shape[0]
    for t in tiles(rows):
        m, _ = unit(x1[t, :])
        a3 = (m * gains[2:3, :]).astype(BF16)
        a3_o[t, :] = a3
        y, slope = gelu_parts(mm(a3, up[...]))
        slope_o[t, :] = slope.astype(BF16)
        rest_o[t, :] = y[:, 0:512]
        mg, rs = unit(y[:, 512:1024])
        mg_o[t, :] = mg
        rs_o[t, :] = rs
        n_o[t, :] = (mg * inner[...]).astype(BF16)
    edge_sends(sc, n_o, ea_o, eb_o)


def mixed_kernel(sc, n, ha, hb, rest, taps, down, mixed_o, gated_o, cat_o, wide):
    rows = n.shape[0]
    fill_wide(sc, wide, (n,), ha, hb)
    conv_fwd(sc, wide, taps, mixed_o, rows)
    for t in tiles(rows):
        gated = (rest[t, :] * mixed_o[t, :]).astype(BF16)
        gated_o[t, :] = gated
        cat_o[t, :] = mm(gated, down[...]).astype(BF16)


def head_masks(rows):
    lane = lax.broadcasted_iota(jnp.int32, (rows, LANES), 1)
    return lane


def query_aug(sc, q, h, lane, utt):
    half = h % 2
    pair = q[:, (h // 2) * LANES : (h // 2 + 1) * LANES].astype(F32)
    off = HEAD_DIM * (1 - half)
    flags = jnp.where((lane == off + utt), 1.0, 0.0)
    mine = (lane >> 6) == half
    return jnp.where(mine, pair, flags).astype(BF16), jnp.where(mine, pair, 0.0).astype(BF16)


def key_bias(sc, src, lane, rows):
    row = lax.broadcasted_iota(jnp.int32, (rows, LANES), 0)
    shift = sc[0] - 1
    utt = row & shift
    pos = (row >> shift) + src * (rows >> shift)
    ok = pos < jnp.where(utt == 0, sc[2], sc[3])
    col = lane & 63
    seen = ok & (col == utt)
    return jnp.where((col < 2) & jnp.logical_not(seen), HIDE, 0.0)


def key_aug(kv, h, lane, bias):
    half = h % 2
    pair = kv[:, (h // 2) * LANES : (h // 2 + 1) * LANES].astype(F32)
    mine = (lane >> 6) == half
    return jnp.where(mine, pair, bias).astype(BF16)


def att_kernel(first, final, masks, sc, q, *rest):
    kvs, rest = rest[: len(masks)], rest[len(masks) :]
    if not first:
        c_i, l_i, acc_i = rest[:3]
        rest = rest[3:]
    if final:
        catg, out_w, c_o, l_o, oT_o, ob_o, att_o, ea_o, eb_o, acc_o = rest
    else:
        c_o, l_o, acc_o = rest
    rows = q.shape[0]
    lane = lax.broadcasted_iota(jnp.int32, (rows, LANES), 1)
    utt = lax.broadcasted_iota(jnp.int32, (rows, LANES), 0) & (sc[0] - 1)
    qs = [query_aug(sc, q, h, lane, utt)[0] for h in range(HEADS)]
    if first:
        c_o[...] = jnp.full((8, rows), -1e30, F32)
        l_o[...] = jnp.zeros((8, rows), F32)
        acc_o[...] = jnp.zeros((HEADS * HEAD_DIM, rows), F32)
    else:
        c_o[...] = c_i[...]
        l_o[...] = l_i[...]
        acc_o[...] = acc_i[...]
    for mask, kv in zip(masks, kvs):
        bias = key_bias(sc, sc[1] ^ mask, lane, rows)
        vT = kv[:, 256:512].astype(F32).T.astype(BF16)
        for h in range(HEADS):
            s = mm_nt(key_aug(kv, h, lane, bias), qs[h])
            old = c_o[h : h + 1, :]
            new = jnp.maximum(old, jnp.floor(jnp.max(s, 0, keepdims=True) * EXP_SCALE))
            w = jnp.exp2(s * EXP_SCALE - new)
            scale = jnp.exp2(old - new)
            c_o[h : h + 1, :] = new
            l_o[h : h + 1, :] = l_o[h : h + 1, :] * scale + jnp.sum(w, 0, keepdims=True)
            hr = slice(h * HEAD_DIM, (h + 1) * HEAD_DIM)
            acc_o[hr, :] = acc_o[hr, :] * scale + mm(vT[hr, :], w.astype(BF16))
    if final:
        for h in range(HEADS):
            hr = slice(h * HEAD_DIM, (h + 1) * HEAD_DIM)
            oT_o[hr, :] = acc_o[hr, :] / l_o[h : h + 1, :]
        ob = oT_o[...].T.astype(BF16)
        ob_o[...] = ob
        att_o[...] = mm(ob, out_w[...]).astype(BF16)
        edge_sends(sc, (att_o, catg), ea_o, eb_o)


def merge_kernel(
    sc, att, catg, ha, hb, x1, taps, mw, dout, gains, w1, w2,
    out_o, un_o, em_o, ec_o, df_o, g2_o, a4_o, h_o, e2_o, du_o, gg_o, ea_o, eb_o, wide, conv,
):
    rows = att.shape[0]
    fill_wide(sc, wide, (att, catg), ha, hb)
    conv_fwd(sc, wide, taps, conv, rows)
    g3g = jnp.zeros((1, 256), F32)
    g4g = jnp.zeros((1, 256), F32)
    for t in tiles(rows):
        cat = jnp.concatenate([att[t, :], catg[t, :]], 1).astype(F32)
        united = (cat + conv[t, :]).astype(BF16)
        un_o[t, :] = united
        x2 = x1[t, :] + mm(united, mw[...])
        m2, rs2 = unit(x2)
        a4 = (m2 * gains[3:4, :]).astype(BF16)
        a4_o[t, :] = a4
        h, d = silu_parts(mm(a4, w1[...]))
        h = h.astype(BF16)
        h_o[t, :] = h
        x3 = x2 + 0.5 * mm(h, w2[...])
        m3, rs3 = unit(x3)
        out_o[t, :] = (m3 * gains[4:5, :]).astype(BF16)
        g3, gg = unit_back(dout[t, :], m3, rs3, gains[4:5, :])
        g4g = g4g + gg
        e2 = (0.5 * g3).astype(BF16)
        e2_o[t, :] = e2
        du = (mm_nt(e2, w2[...]) * d).astype(BF16)
        du_o[t, :] = du
        back, gg = unit_back(mm_nt(du, w1[...]), m2, rs2, gains[3:4, :])
        g3g = g3g + gg
        g2 = g3 + back
        g2_o[t, :] = g2
        em = g2.astype(BF16)
        em_o[t, :] = em
        df = mm_nt(em, mw[...])
        df_o[t, :] = df
        ec_o[t, :] = df.astype(BF16)
    gg_o[...] = jnp.concatenate([g3g, g4g, jnp.zeros((6, 256), F32)], 0)
    edge_sends(sc, ec_o, ea_o, eb_o)


def put_cols(buf, row, value):
    n = value.shape[0]
    for c in range(value.shape[1] // 256):
        buf[row + c * n : row + (c + 1) * n, :] = value[:, c * 256 : (c + 1) * 256].astype(BF16)


def grads_kernel(a4, h, e2, du, un, em, buf):
    put_cols(buf, 0, mm_tn(a4[...], du[...]))
    put_cols(buf, 1024, mm_tn(h[...], e2[...]))
    put_cols(buf, 2048, mm_tn(un[...], em[...]))


def split_kernel(
    sc, ec, ha, hb, df, att, catg, rest, mixed, oT, l, taps, down, out_w,
    eatt_o, ecg_o, emix_o, dm_o, eaT_o, ean_o, del_o, tg_o, ea_o, eb_o, wide, conv, catf,
):
    rows = ec.shape[0]
    fill_wide(sc, wide, (ec,), ha, hb)
    conv[...] = df[...]
    catf[:, 0:256] = att[...].astype(F32)
    catf[:, 256:512] = catg[...].astype(F32)
    tg_o[...] = jnp.zeros((32, 512), F32)
    conv_back(sc, wide, taps, catf, conv, tg_o, rows)
    for t in tiles(rows):
        eatt_o[t, :] = conv[t, 0:256].astype(BF16)
        ecg = conv[t, 256:512].astype(BF16)
        ecg_o[t, :] = ecg
        dg = mm_nt(ecg, down[...])
        emix_o[t, :] = (dg * rest[t, :]).astype(BF16)
        dm_o[t, :] = dg * mixed[t, :]
    edge_sends(sc, emix_o, ea_o, eb_o)
    doT = mm_nt(out_w[...], eatt_o[...])
    del_o[...] = jnp.zeros((8, rows), F32)
    for h in range(HEADS):
        hr = slice(h * HEAD_DIM, (h + 1) * HEAD_DIM)
        inv = 1.0 / l[h : h + 1, :]
        eaT = (doT[hr, :] * inv).astype(BF16)
        eaT_o[hr, :] = eaT
        del_o[h : h + 1, :] = jnp.sum(doT[hr, :] * oT[hr, :], 0, keepdims=True) * inv
    ean_o[...] = eaT_o[...].astype(F32).T.astype(BF16)


def attback_kernel(first, masks, sc, q, *rest):
    kvs, rest = rest[: len(masks)], rest[len(masks) :]
    c, eaT, ean, delta = rest[:4]
    rest = rest[4:]
    if first:
        dq_i = None
    else:
        dq_i, rest = rest[0], rest[1:]
    dq_o, d_os = rest[0], rest[1:]
    rows = q.shape[0]
    lane = lax.broadcasted_iota(jnp.int32, (rows, LANES), 1)
    utt = lax.broadcasted_iota(jnp.int32, (rows, LANES), 0) & (sc[0] - 1)
    sub = lax.broadcasted_iota(jnp.int32, (LANES, rows), 0)
    if first:
        dq_o[...] = jnp.zeros((HEADS * HEAD_DIM, rows), F32)
    else:
        dq_o[...] = dq_i[...]
    for mask, kv, d_o in zip(masks, kvs, d_os):
        bias = key_bias(sc, sc[1] ^ mask, lane, rows)
        kT = kv[:, 0:256].astype(F32).T.astype(BF16)
        for pair in range(HEADS // 2):
            cols = slice(pair * LANES, (pair + 1) * LANES)
            vcols = slice(256 + pair * LANES, 256 + (pair + 1) * LANES)
            dk = jnp.zeros((rows, LANES), F32)
            dv = jnp.zeros((rows, LANES), F32)
            for half in range(2):
                h = pair * 2 + half
                hr = slice(h * HEAD_DIM, (h + 1) * HEAD_DIM)
                mine = (lane >> 6) == half
                qa, qm = query_aug(sc, q, h, lane, utt)
                s = mm_nt(key_aug(kv, h, lane, bias), qa)
                w = jnp.exp2(s * EXP_SCALE - c[h : h + 1, :])
                eaTm = jnp.where((sub >> 6) == half, eaT[cols, :].astype(F32), 0.0).astype(BF16)
                dp = mm(kv[:, vcols], eaTm)
                ds = (w * (dp - delta[h : h + 1, :])).astype(BF16)
                eam = jnp.where(mine, ean[:, cols].astype(F32), 0.0).astype(BF16)
                dk = dk + mm(ds, qm)
                dv = dv + mm(w.astype(BF16), eam)
                dq_o[hr, :] += mm(kT[hr, :], ds)
            d_o[:, cols] = (dk * SCORE_SCALE).astype(d_o.dtype)
            d_o[:, vcols] = dv.astype(d_o.dtype)


def gateback_kernel(
    sc, emix, ha, hb, n, mg, rs, dm, slope, a3, x1, gated, ecg, ob, eatt, taps, inner, up, gains,
    bcg_o, gg_o, tg_o, gi_o, buf, wide, conv,
):
    rows = emix.shape[0]
    fill_wide(sc, wide, (emix,), ha, hb)
    conv[...] = jnp.zeros_like(conv)
    tg_o[...] = jnp.zeros((32, 512), F32)
    conv_back(sc, wide, taps, n, conv, tg_o, rows)
    gi = jnp.zeros((1, 512), F32)
    gc = jnp.zeros((1, 256), F32)
    ups = []
    for t in tiles(rows):
        dgate, g = unit_back(conv[t, :], mg[t, :], rs[t, :], inner[...])
        gi = gi + g
        sl = slope[t, :].astype(F32)
        eup = jnp.concatenate([dm[t, :] * sl[:, 0:512], dgate * sl[:, 512:1024]], 1).astype(BF16)
        ups.append(eup)
        m, rs1 = unit(x1[t, :])
        back, g = unit_back(mm_nt(eup, up[...]), m, rs1, gains[2:3, :])
        gc = gc + g
        bcg_o[t, :] = back
    gi_o[...] = jnp.concatenate([gi, jnp.zeros((7, 512), F32)], 0)
    gg_o[...] = jnp.concatenate([gc, jnp.zeros((7, 256), F32)], 0)
    eup = jnp.concatenate(ups, 0)
    put_cols(buf, 0, mm_tn(a3[...], eup))
    put_cols(buf, 1024, mm_tn(gated[...], ecg[...]))
    put_cols(buf, 1536, mm_tn(ob[...], eatt[...]))


def last_kernel(
    sc, dqT, dkv0, dkv1, dkv2, a2, x1, g2, bcg, a1, h, d, freq, wq, gains, feat, w1, w2,
    dx_o, gg_o, buf,
):
    rows = x1.shape[0]
    cos, sin = turn_tables(sc, freq[...], rows)
    dq = dqT[...].T * SCORE_SCALE
    g0 = jnp.zeros((1, 256), F32)
    g1g = jnp.zeros((1, 256), F32)
    eqkvs, e1s, dus = [], [], []
    for t in tiles(rows):
        dkv = dkv0[t, :] + dkv1[t, :].astype(F32) + dkv2[t, :].astype(F32)
        eq = rotate(dq[t], cos[t], sin[t], -1.0).astype(BF16)
        ek = rotate(dkv[:, 0:256], cos[t], sin[t], -1.0).astype(BF16)
        eqkv = jnp.concatenate([eq, ek, dkv[:, 256:512].astype(BF16)], 1)
        eqkvs.append(eqkv)
        m, rs = unit(x1[t, :])
        back, g = unit_back(mm_nt(eqkv, wq[...]), m, rs, gains[1:2, :])
        g1g = g1g + g
        g1 = g2[t, :] + back + bcg[t, :]
        e1 = (0.5 * g1).astype(BF16)
        e1s.append(e1)
        du = (mm_nt(e1, w2[...]) * d[t, :].astype(F32)).astype(BF16)
        dus.append(du)
        keep = keep_mask(sc, t.start, (t.stop - t.start, 256))
        m, rs = unit(jnp.where(keep, feat[t, :].astype(F32), 0.0))
        back, g = unit_back(mm_nt(du, w1[...]), m, rs, gains[0:1, :])
        g0 = g0 + g
        dx_o[t, :] = jnp.where(keep, g1 + back, 0.0)
    gg_o[...] = jnp.concatenate([g0, g1g, jnp.zeros((6, 256), F32)], 0)
    put_cols(buf, 0, mm_tn(a1[...], jnp.concatenate(dus, 0)))
    put_cols(buf, 1024, mm_tn(h[...], jnp.concatenate(e1s, 0)))
    put_cols(buf, 2048, mm_tn(a2[...], jnp.concatenate(eqkvs, 0)))


def join_kernel(left, right, out):
    out[...] = (left[...].astype(F32) + right[...].astype(F32)).astype(BF16)


def rank():
    return lax.axis_index("grp") * lax.axis_size("blk") + lax.axis_index("blk")


def pack_kernel(p1, p2, p3, tg_gate, tg_merge, gi, gg01, gg2, gg34, keep, send, extra):
    half = keep.shape[0]
    extra[0:32, :] = tg_gate[:, 0:256].astype(BF16)
    extra[32:64, :] = tg_gate[:, 256:512].astype(BF16)
    extra[64:96, :] = tg_merge[:, 0:256].astype(BF16)
    extra[96:128, :] = tg_merge[:, 256:512].astype(BF16)
    small = [gg01[0:2, :], gg2[0:1, :], gg34[0:2, :], gi[0:1, 0:256], gi[0:1, 256:512], jnp.zeros((9, 256), F32)]
    extra[128:144, :] = jnp.concatenate(small, 0).astype(BF16)
    extra[144:, :] = jnp.zeros((extra.shape[0] - 144, 256), BF16)
    spans = []
    start = 0
    for ref in (p1, p2, p3, extra):
        n = ref.shape[0]
        for j in range(2):
            low, high = max(start, j * half), min(start + n, (j + 1) * half)
            if low < high:
                spans.append((ref, j, low - start, low - j * half, high - low))
        start += n
    bit = rank() % 2
    for own in range(2):

        @pl.when(bit == own)
        def _():
            for ref, j, at, to, n in spans:
                dst = keep if j == own else send
                dst[to : to + n, :] = ref[at : at + n, :]


def slot_bit(pair):
    index = rank()
    mask = jnp.where(index % 2 == 0, pair[0], pair[1])
    return (index // mask) % 2


def fold_kernel(pair, mine, got, *outs):
    if pair is None:
        outs[0][...] = (mine[...].astype(F32) + got[...].astype(F32)).astype(BF16)
        return
    keep, send = outs
    half = keep.shape[0]
    bit = slot_bit(pair)
    for ref, b in ((send, 1 - bit), (keep, bit)):
        here = pl.ds(pl.multiple_of(b * half, 16), half)
        ref[...] = (mine[here, :].astype(F32) + got[here, :].astype(F32)).astype(BF16)


def grow_kernel(pair, mine, got, out):
    half = mine.shape[0]
    bit = slot_bit(pair)
    out[pl.ds(pl.multiple_of(bit * half, 16), half), :] = mine[...]
    out[pl.ds(pl.multiple_of((1 - bit) * half, 16), half), :] = got[...]


def unpack_kernel(layout, mine, got, *refs):
    count = len(layout)
    outs, bufs, whole, sems = refs[:count], refs[count : 2 * count], refs[2 * count], refs[2 * count + 1]
    half = mine.shape[0]
    bit = rank() % 2
    whole[pl.ds(pl.multiple_of(bit * half, 16), half), :] = mine[...]
    whole[pl.ds(pl.multiple_of((1 - bit) * half, 16), half), :] = got[...]
    copies = []
    for i, (row, n, cols) in enumerate(layout):
        buf = bufs[i]
        if n == 5:
            buf[...] = whole[row : row + 16, :].astype(F32)[0:5, :]
        elif n == 1:
            v = whole[row - 5 : row + 11, :].astype(F32)
            buf[0:1, 0:256] = v[5:6, :]
            buf[0:1, 256:512] = v[6:7, :]
        else:
            full = -(-n // 16) * 16
            for c in range(cols // 256):
                v = whole[row + c * full : row + (c + 1) * full, :].astype(F32)
                buf[:, c * 256 : (c + 1) * 256] = v[0:n, :]
        copies.append(pltpu.make_async_copy(buf, outs[i], sems.at[i]))
        copies[-1].start()
    for copy in copies:
        copy.wait()


def small_call(kernel, outs, ins, us, scratch=(), limit=None, out_space=None):
    vmem = pl.BlockSpec(memory_space=pltpu.VMEM)
    return pl.pallas_call(
        kernel,
        out_shape=[jax.ShapeDtypeStruct(s, d) for s, d in outs],
        in_specs=[vmem] * len(ins),
        out_specs=[vmem if out_space is None else pl.BlockSpec(memory_space=out_space)] * len(outs),
        scratch_shapes=list(scratch),
        compiler_params=pltpu.CompilerParams(vmem_limit_bytes=limit or VMEM_BYTES),
        cost_estimate=pl.CostEstimate(flops=int(us * UNIT), bytes_accessed=1, transcendentals=0),
    )(*ins)


def reduce_all(keep, send, layout):
    grp, blk = lax.axis_size("grp"), lax.axis_size("blk")
    count = grp * blk
    width = keep.shape[1]
    masks = [1 << i for i in range(1, count.bit_length() - 1)]
    first = list(masks)
    second = list(masks)
    if len(masks) > 2:
        first[1], first[2] = first[2], first[1]
        second[0], second[1] = second[1], second[0]
    slots = list(zip(first, second))

    def exchange(value, pair):
        return lax.ppermute(value, AXES, [(i, i ^ pair[i % 2]) for i in range(count)])

    got = exchange(send, (1, 1))
    for pair in slots:
        half = keep.shape[0] // 2
        outs = [((half, width), BF16)] * 2
        keep, send = small_call(functools.partial(fold_kernel, pair), outs, [keep, got], 0.5)
        got = exchange(send, pair)
    (mine,) = small_call(functools.partial(fold_kernel, None), [(keep.shape, BF16)], [keep, got], 0.3)
    for pair in reversed(slots):
        got = exchange(mine, pair)
        shape = (2 * mine.shape[0], width)
        (mine,) = small_call(functools.partial(grow_kernel, pair), [(shape, BF16)], [mine, got], 0.4)
    got = exchange(mine, (1, 1))
    shapes = [(n, cols) for _, n, cols in layout]
    return small_call(
        functools.partial(unpack_kernel, layout), [(s, F32) for s in shapes], [mine, got], 3.0,
        [pltpu.VMEM(s, F32) for s in shapes]
        + [pltpu.VMEM((2 * mine.shape[0], width), BF16), pltpu.SemaphoreType.DMA((len(shapes),))],
        32 * 1024 * 1024, pltpu.HBM,
    )


def plain(kernel, ins, outs, kept, *refs):
    head = refs[: ins]
    made = refs[ins + kept : ins + kept + outs]
    scratch = refs[ins + 2 * kept + outs :]
    kernel(*head, *made, *scratch)


class Layer:
    def __init__(self, plan):
        self.plan = plan
        self.step = 0
        self.have = {}

    def __getitem__(self, key):
        return self.have[key]

    def __setitem__(self, key, value):
        self.have[key] = value

    def run(self, kernel, outs, extra=(), scratch=(), us=1.0):
        name, reads = self.plan[self.step]
        later = [r for _, more in self.plan[self.step + 1 :] for r in more]
        kept = sorted(k for k in self.have if k in later and k not in reads and k != "sc")
        self.step += 1
        smem = pl.BlockSpec(memory_space=pltpu.SMEM)
        vmem = pl.BlockSpec(memory_space=pltpu.VMEM)
        ins = [self.have[r] for r in reads] + list(extra)
        in_specs = [smem if r == "sc" else vmem for r in reads] + [vmem] * len(extra)
        shapes = [jax.ShapeDtypeStruct(s, d) for _, s, d in outs]
        shapes += [jax.ShapeDtypeStruct(self.have[k].shape, self.have[k].dtype) for k in kept]
        made = pl.pallas_call(
            functools.partial(plain, kernel, len(ins), len(outs), len(kept)),
            out_shape=shapes,
            in_specs=in_specs + [vmem] * len(kept),
            out_specs=[vmem] * len(shapes),
            scratch_shapes=list(scratch),
            input_output_aliases={len(ins) + i: len(outs) + i for i in range(len(kept))},
            compiler_params=pltpu.CompilerParams(vmem_limit_bytes=VMEM_BYTES),
            cost_estimate=pl.CostEstimate(flops=int(us * UNIT), bytes_accessed=1, transcendentals=0),
            name=name,
        )(*ins, *[self.have[k] for k in kept])
        for key, value in zip([o[0] for o in outs] + kept, made):
            self.have[key] = value


def swap(value, axis, mask):
    count = math.prod(lax.axis_size(a) for a in axis) if isinstance(axis, tuple) else lax.axis_size(axis)
    return lax.ppermute(value, axis, [(i, i ^ mask) for i in range(count)])


def halo(ea, eb):
    count = lax.axis_size("blk")
    near = [(i, i ^ 1) for i in range(count)]
    far = []
    for i in range(1, count - 1, 2):
        far += [(i, i + 1), (i + 1, i)]
    return lax.ppermute(ea, "blk", near), lax.ppermute(eb, "blk", far)


def local(
    features, d_out, bucket_batch, valid_len, time_start, time_width, freq_start, freq_width,
    gains, inner_gain, ffn1_in, ffn1_out, qkv_w, out_w, cg_up, cg_conv, cg_down, merge_conv,
    merge_w, ffn2_in, ffn2_out,
):
    rows, width = features.shape
    half = cg_down.shape[0]
    ff = ffn1_in.shape[1]
    blocks = lax.axis_size("blk")
    me = lax.axis_index("blk")
    freq = np.exp(np.arange(32, dtype=np.float64) * (-2.0 * math.log(10000.0) / HEAD_DIM))
    freq = jnp.asarray(np.tile(freq, 4)[None, :].astype(np.float32))
    wide = pltpu.VMEM((half // LANES, rows + 2 * HALO, LANES), F32)
    plane = pltpu.VMEM((rows, half), F32)
    pairs = [(m, m | 1) for m in range(0, blocks, 2)]
    kvs = [(f"kv{a}", f"kv{b}") for a, b in pairs]
    even = [a for a, _ in pairs[1:]]
    state = ["c", "l", "acc"]
    plan = [("gate", ["sc", "x1"])]
    plan += [("att_first", ["sc", "q", *kvs[0]])]
    plan += [("mixed", ["sc", "n", "na", "nb", "rest"])]
    far_masks = [m for a, b in pairs[1:] for m in (a, b)]
    plan += [("att_mid", ["sc", "q", f"kv{m}", *state]) for m in far_masks[:-1]]
    plan += [
        ("att_last", ["sc", "q", f"kv{far_masks[-1]}", *state, "catg"]),
        ("merge", ["sc", "att", "catg", "ha", "hb", "x1"]),
        ("grads2", ["a4", "h2", "e2", "du2", "un", "em"]),
        ("split", ["sc", "ec", "ca", "cb", "df", "att", "catg", "rest", "mixed", "oT", "l"]),
    ]
    back = ["c", "eaT", "ean", "delta"]
    for e in even:
        for m in (e + 1, e):
            plan += [("attback", ["sc", "q", f"kv{m}", *back] + (["dqT"] if m != even[0] + 1 else []))]
        plan += [("join_kv", [f"pd{e}", f"in{e}"])]
    plan += [("attback", ["sc", "q", "kv1", "kv0", *back, "dqT"])]
    plan += [
        ("gateback", ["sc", "emix", "ma", "mb", "n", "mg", "rs", "dm", "slope", "a3", "x1", "gated", "ecg", "ob", "eatt"]),
    ]
    total = f"far{even[0]}"
    for e in even[1:]:
        plan += [("join_far", [total, f"far{e}"])]
        total = f"t{e}"
    plan += [
        ("last", ["sc", "dqT", "own", "near", total, "a2", "x1", "g2", "bcg", "a1", "h1", "d1"]),
        ("pack", ["part1", "buf2", "buf3", "tg_gate", "tg_merge", "gi", "gg01", "gg2", "gg34"]),
    ]
    run = Layer(plan)
    smem = pl.BlockSpec(memory_space=pltpu.SMEM)
    vmem = pl.BlockSpec(memory_space=pltpu.VMEM)
    raw = (bucket_batch, valid_len, time_start, time_width, freq_start, freq_width, gains, freq,
           features, ffn1_in, ffn1_out, qkv_w)
    def narrow(name, kind=BF16):
        return (name, (rows, width), kind)

    def middle(name, kind=BF16):
        return (name, (rows, half), kind)

    def broad(name, kind=BF16):
        return (name, (rows, ff), kind)

    outs = [narrow("x1", F32), narrow("a1"), broad("h1"), broad("d1"), narrow("a2"), narrow("q"), middle("kv0"), middle("kvs")]
    made = pl.pallas_call(
        pre_kernel,
        out_shape=[jax.ShapeDtypeStruct((16,), jnp.int32)] + [jax.ShapeDtypeStruct(o[1], o[2]) for o in outs],
        in_specs=[pl.BlockSpec(memory_space=pltpu.HBM)] * 12,
        out_specs=[smem] + [vmem] * 8,
        scratch_shapes=[pltpu.SMEM(v.shape, v.dtype) for v in raw[:6]]
        + [pltpu.VMEM(v.shape, v.dtype) for v in raw[6:]] + [pltpu.SemaphoreType.DMA((12,))],
        compiler_params=pltpu.CompilerParams(vmem_limit_bytes=VMEM_BYTES),
        cost_estimate=pl.CostEstimate(flops=int(4.0 * UNIT), bytes_accessed=1, transcendentals=0),
        name="pre",
    )(raw[0], *[pltpu.with_memory_space_constraint(v, pltpu.HBM) for v in raw[1:]])
    for key, value in zip(["sc"] + [o[0] for o in outs], made):
        run[key] = value
    held = {0: run["kvs"]}
    bit = blocks // 2
    while bit > 1:
        held.update({m | bit: swap(held[m], "blk", bit) for m in list(held)})
        bit //= 2
    held[1] = swap(held[0], "blk", 1)

    def send_edges():
        return halo(run["ea"], run["eb"])

    edge = [("ea", (HALO, half), BF16), ("eb", (HALO, half), BF16)]
    stats = [("c", (8, rows), F32), ("l", (8, rows), F32)]

    run.run(
        gate_kernel,
        [narrow("a3"), middle("rest", F32), broad("slope"), middle("n"), middle("mg", F32), ("rs", (rows, 1), F32)] + edge,
        [gains, inner_gain[None, :], cg_up], us=2.5,
    )
    edges = send_edges()
    run["kv1"] = held[1]
    run.run(functools.partial(att_kernel, True, False, pairs[0]), stats + [("acc", (width, rows), F32)], us=0.5)
    run["na"], run["nb"] = edges
    run.run(
        mixed_kernel, [middle("mixed", F32), middle("gated"), narrow("catg")],
        [cg_conv, cg_down], [wide], us=5.3,
    )
    for a, b in pairs[1:]:
        late, _ = lax.optimization_barrier((held[a], run["catg"]))
        run[f"kv{a}"] = late
        mate = swap(late, "blk", 1)
        run.run(
            functools.partial(att_kernel, False, False, (a,)), stats + [("acc", (width, rows), F32)], us=2.8,
        )
        run[f"kv{b}"] = mate
        if b < blocks - 1:
            run.run(
                functools.partial(att_kernel, False, False, (b,)), stats + [("acc", (width, rows), F32)], us=2.8,
            )
    run.run(
        functools.partial(att_kernel, False, True, (blocks - 1,)),
        stats + [("oT", (width, rows), F32), narrow("ob"), narrow("att")] + edge,
        [out_w], [pltpu.VMEM((width, rows), F32)], us=3.0,
    )
    run["ha"], run["hb"] = send_edges()
    run.run(
        merge_kernel,
        [narrow("out"), middle("un"), narrow("em"), middle("ec"), middle("df", F32), narrow("g2", F32), narrow("a4"),
         broad("h2"), narrow("e2"), broad("du2"), ("gg34", (8, width), F32)] + edge,
        [merge_conv, merge_w, d_out, gains, ffn2_in, ffn2_out], [wide, plane], us=9.1,
    )
    edges = send_edges()
    run.run(grads_kernel, [("part1", (2560, width), BF16)], us=0.9)
    run["ca"], run["cb"] = edges
    run.run(
        split_kernel,
        [narrow("eatt"), narrow("ecg"), middle("emix"), middle("dm", F32), ("eaT", (width, rows), BF16), narrow("ean"),
         ("delta", (8, rows), F32), ("tg_merge", (32, half), F32)] + edge,
        [merge_conv, cg_down, out_w], [wide, plane, plane], us=8.3,
    )
    edges = send_edges()

    tall = ("dqT", (width, rows), F32)
    pair_sum = (rows, 2 * width)
    for e in even:
        for m in (e + 1, e):
            run.run(
                functools.partial(attback_kernel, m == even[0] + 1, (m,)), [tall, (f"pd{m}", pair_sum, BF16)], us=0.5
            )
            if m == even[0] + 1:
                run["ma"], run["mb"] = edges
            if m & 1:
                arrival = swap(run[f"pd{m}"], "blk", 1)
        run[f"in{e}"] = arrival
        run.run(join_kernel, [(f"s{e}", pair_sum, BF16)], us=0.2)
    fars = {e: swap(run[f"s{e}"], "blk", e) for e in even}
    run.run(
        functools.partial(attback_kernel, False, (1, 0)), [tall, ("pd1", pair_sum, BF16), ("own", pair_sum, F32)], us=6.3
    )
    near = swap(run["pd1"], "blk", 1)
    run.run(
        gateback_kernel,
        [narrow("bcg", F32), ("gg2", (8, width), F32), ("tg_gate", (32, half), F32), ("gi", (8, half), F32),
         ("buf2", (1792, width), BF16)],
        [cg_conv, inner_gain[None, :], cg_up, gains], [wide, plane], us=1.0,
    )
    run["near"] = near
    for e in even:
        run[f"far{e}"] = fars[e]
    for e in even[1:]:
        run.run(join_kernel, [(f"t{e}", pair_sum, BF16)], us=0.2)
    run.run(
        last_kernel,
        [narrow("dx", F32), ("gg01", (8, width), F32), ("buf3", (2816, width), BF16)],
        [freq, qkv_w, gains, features, ffn1_in, ffn1_out], us=4.2,
    )
    count = lax.axis_size("grp") * blocks
    used = 2560 + 1792 + 2816 + 144
    total = -(-used // (16 * count)) * 16 * count
    run.run(
        pack_kernel, [("keep", (total // 2, width), BF16), ("send", (total // 2, width), BF16)],
        (), [pltpu.VMEM((total - used + 144, width), BF16)], us=1.0,
    )
    layout = (
        (7296, 5, 256), (7301, 1, 512), (4352, 256, 1024), (5376, 1024, 256), (6400, 256, 768), (4096, 256, 256),
        (2560, 256, 1024), (7168, 31, 512), (3584, 512, 256), (7232, 31, 512), (2048, 512, 256), (0, 256, 1024),
        (1024, 1024, 256),
    )
    sums = reduce_all(run["keep"], run["send"], layout)
    return (run["out"], run["dx"], sums[0], sums[1][0], *sums[2:])


def solution(mesh):
    rows = P(("grp", "blk"), None)
    in_specs = (rows, rows, P("grp")) + (P("grp", None),) * 5 + (P(),) * 13
    out_specs = (rows, rows) + (P(),) * 13
    return jax.shard_map(local, mesh=mesh, in_specs=in_specs, out_specs=out_specs, check_vma=False)
```

time: 644 us -> 193 us (0.30)
  waiting for transfers between devices: 332 us -> 70.7 us
  other arithmetic: 98.4 us -> 0 us
  matrix products: 88 us -> 0 us
  Pallas kernels: 0 us -> 75.1 us
  local copies, waits for them, and re-layouts: 58.6 us -> 0.08 us
  between operations: 18.3 us -> 2.04 us
    psum x2 -> x0, waiting for transfers between devices: 302 us -> none  [local(): lax.psum((jnp.stack([grad_first_gain, grad_att_gain, grad_cg_gain, grad_s...]
    dot_general x55 -> x0, matrix products: 88 us -> none  [the longest x9 18.9 us: product_t(): lax.dot_general(left, right, (((1,), (1,)), ((), ())), preferred_element_...]
    pallas_call x0 -> x26, Pallas kernels: none -> 75.1 us  [the longest x15 66.3 us: run(): pl.pallas_call(functools.partial(plain, kernel, len(ins), len(outs), len(...]
    ppermute x24, waiting for transfers between devices: 30.5 us -> 70.7 us  [the longest x10 66.5 us: exchange(): lax.ppermute(value, AXES, [(i, i ^ pair[i % 2]) for i in range(count)])]
    convert_element_type x17 -> x0, other arithmetic: 38.7 us -> none  [the longest x6 25.3 us: to_half(): return value.astype(jnp.bfloat16)]
    reduce_sum x23 -> x0, other arithmetic: 31.2 us -> none  [the longest x2 13.7 us: norm_backward(): gain_grad = jnp.sum(upstream * unit_part, 0)]
    unnamed x402 -> x32, local copies, waits for them, and re-layouts: 30.1 us -> 0.08 us
    another operation x8 -> x0, other arithmetic: 14.4 us -> none
  transfers between devices with their start and end apart: 26 -> 24, of which waited for: 18 -> 13; matrix products, arithmetic and copies ran while one was open for 20% -> 0% of each run, Pallas kernels for 0% -> 16%
where the time goes in v1:
time: 193 us; the launch traced here: 189 us
  Pallas kernels  75.1 us (39%)
  waiting for transfers between devices  70.7 us (37%)
  starting transfers between devices  40.9 us (21%)
  between operations  2.04 us (1%)
    ppermute x10, waiting for transfers between devices, exchange(): lax.ppermute(value, AXES, [(i, i ^ pair[i % 2]) for i in range(count)])  66.5 us
    pallas_call x15, Pallas kernels, run(): pl.pallas_call(functools.partial(plain, kernel, len(ins), len(outs), len(...  66.3 us
    ppermute x6, starting transfers between devices, swap(): return lax.ppermute(value, axis, [(i, i ^ mask) for i in range(count)])  16.2 us
    ppermute x10, starting transfers between devices, exchange(): lax.ppermute(value, AXES, [(i, i ^ pair[i % 2]) for i in range(count)])  16 us
    ppermute x8, starting transfers between devices, halo(): return (lax.ppermute(ea, 'blk', near), lax.ppermute(eb, 'blk', far))  8.68 us
    pallas_call x10, Pallas kernels, small_call(): pl.pallas_call(kernel, out_shape=[jax.ShapeDtypeStruct(s, d) for s, d in...  4.74 us
    pallas_call x1, Pallas kernels, local(): pl.pallas_call(pre_kernel, out_shape=[jax.ShapeDtypeStruct((16,), jnp.int...  4.12 us
  transfers between devices with their start and end apart: 24, of which 13 were waited for; matrix products, arithmetic and copies ran while one was open for 0% of the time, Pallas kernels for 16%

profile of v1, /device:TPU:0, one launch (start us, length us, event | category | flops | bytes accessed | tf_op | source)
XLA Modules:
  0.0 188.8 jit_solution(15145097705411943570)
XLA Ops:
  1.3 4.1 %pre.1 = (s32[16]{0:T(128)S(1)}, f32[512,256]{1,0:T(8,128)S(1)}, bf16[512,256]{1,0:T(8,128)(2,1)S(1)}, bf16[512,1024]{1,0:T(8,128)(2,1)S(1)}, bf16[512,1024]{1,0...) custom-call(s32[1]{0:T(128)S(6)} %copy.537.refs_0_, ...), custom_call_target="tpu_custom_call" | custom-call | flops 1400000000 | bytes 1 | tf_op jit(solution)/shard_map/pre/pallas_call | solution.py:811
  5.5 0.5 collective-permute-start
  6.0 2.6 %collective-permute-start.3 = (bf16[512,512]{1,0:T(8,128)(2,1)S(1)}, bf16[512,512]{1,0:T(8,128)(2,1)S(1)}, u32[]{:S(2)}, u32[]{:S(2)}) collective-permute-start(bf16[512,512]{1,0:T(8,128)(2,1)S(1)} %get-tuple-element.372), channel_id=1, source_target_pairs={{0,2},{1,3},{2,0},{3,1},{4,6},{5,7},{6,4},{7,5},{8,10},{9,11},{10,... | collective-permute-start | bytes 1572872 | tf_op jit(solution)/shard_map/ppermute | solution.py:738
  8.5 2.5 %gate.1 = (bf16[512,256]{1,0:T(8,128)(2,1)S(1)}, f32[512,512]{1,0:T(8,128)S(1)}, bf16[512,1024]{1,0:T(8,128)(2,1)S(1)}, bf16[512,512]{1,0:T(8,128)(2,1)S(1)}, f3...) custom-call(s32[16]{0:T(128)S(1)} %get-tuple-element.362.refs_0_, ...), custom_call_target="tpu_custom_call", output_to_operand_aliasing={{8}: (5, {}), {9}: (6, {}), {10}: (7, {}), {11}: (8, {}), {... | custom-call | flops 875000000 | bytes 1 | tf_op jit(solution)/shard_map/gate/pallas_call | solution.py:721
  11.0 0.2 collective-permute-start.1
  11.3 1.2 collective-permute-start.2
  12.5 0.0 copy-start.1
  12.5 5.2 %att_first.1 = (f32[8,512]{1,0:T(8,128)S(1)}, f32[8,512]{1,0:T(8,128)S(1)}, f32[256,512]{1,0:T(8,128)S(1)}, bf16[512,256]{1,0:T(8,128)(2,1)S(1)}, bf16[512,256]{...) custom-call(s32[16]{0:T(128)S(1)} %get-tuple-element.362.refs_0_, ...), custom_call_target="tpu_custom_call", output_to_operand_aliasing={{3}: (4, {}), {4}: (5, {}), {5}: (6, {}), {6}: (7, {}), {7}... | custom-call | flops 175000000 | bytes 1 | tf_op jit(solution)/shard_map/att_first/pallas_call | solution.py:721
  17.7 5.7 %mixed.1 = (f32[512,512]{1,0:T(8,128)S(1)}, bf16[512,512]{1,0:T(8,128)(2,1)S(1)}, bf16[512,256]{1,0:T(8,128)(2,1)S(1)}, bf16[512,256]{1,0:T(8,128)(2,1)S(1)}, bf...) custom-call(s32[16]{0:T(128)S(1)} %get-tuple-element.362.refs_0_, ...), custom_call_target="tpu_custom_call", output_to_operand_aliasing={{3}: (7, {}), {4}: (8, {}), {5}: (9, {}), {6}: (10, {}), {7... | custom-call | flops 1855000064 | bytes 1 | tf_op jit(solution)/shard_map/mixed/pallas_call | solution.py:721
  23.4 3.5 %collective-permute-start.4 = (bf16[512,512]{1,0:T(8,128)(2,1)S(1)}, bf16[512,512]{1,0:T(8,128)(2,1)S(1)}, u32[]{:S(2)}, u32[]{:S(2)}) collective-permute-start(bf16[512,512]{1,0:T(8,128)(2,1)S(1)} %collective-permute-done.3.refs_2_.refs_16_), channel_id=1, source_target_pairs={{0,1},{1,0},{2,3},{3,2},{4,5},{5,4},{6,7},{7,6},{8,9},{9,8},{10,11... | collective-permute-start | bytes 1572872 | tf_op jit(solution)/shard_map/ppermute | solution.py:738
  27.0 2.9 %att_mid.1 = (f32[8,512]{1,0:T(8,128)S(1)}, f32[8,512]{1,0:T(8,128)S(1)}, f32[256,512]{1,0:T(8,128)S(1)}, bf16[512,256]{1,0:T(8,128)(2,1)S(1)}, bf16[512,256]{1,...) custom-call(s32[16]{0:T(128)S(1)} %get-tuple-element.362.refs_0_, ...), custom_call_target="tpu_custom_call", output_to_operand_aliasing={{3}: (6, {}), {4}: (7, {}), {5}: (8, {}), {6}: (9, {}), {7}... | custom-call | flops 980000000 | bytes 1 | tf_op jit(solution)/shard_map/att_mid/pallas_call | solution.py:721
  29.9 0.0 copy-start.3
  30.0 3.4 %att_last.1 = (f32[8,512]{1,0:T(8,128)S(1)}, f32[8,512]{1,0:T(8,128)S(1)}, f32[256,512]{1,0:T(8,128)S(1)}, bf16[512,256]{1,0:T(8,128)(2,1)S(1)}, bf16[512,256]{1...) custom-call(s32[16]{0:T(128)S(1)} %get-tuple-element.362.refs_0_, ...), custom_call_target="tpu_custom_call", output_to_operand_aliasing={{7}: (8, {}), {8}: (9, {}), {9}: (10, {}), {10}: (11, {}), ... | custom-call | flops 1050000000 | bytes 1 | tf_op jit(solution)/shard_map/att_last/pallas_call | solution.py:721
  33.4 0.1 collective-permute-start.5
  33.5 0.8 collective-permute-start.6
  34.3 0.3 collective-permute-done.5.refs_3_
  34.7 10.0 %merge.1 = (bf16[512,256]{1,0:T(8,128)(2,1)}, bf16[512,512]{1,0:T(8,128)(2,1)S(1)}, bf16[512,256]{1,0:T(8,128)(2,1)S(1)}, bf16[512,512]{1,0:T(8,128)(2,1)S(1)}, ...) custom-call(s32[16]{0:T(128)S(1)} %get-tuple-element.362.refs_0_, ...), custom_call_target="tpu_custom_call", output_to_operand_aliasing={{13}: (12, {}), {14}: (13, {}), {15}: (14, {}), {16}: (15, ... | custom-call | flops 3184999936 | bytes 1 | tf_op jit(solution)/shard_map/merge/pallas_call | solution.py:721
  44.7 4.7 %collective-permute-start.7 = (bf16[32,512]{1,0:T(8,128)(2,1)S(1)}, bf16[32,512]{1,0:T(8,128)(2,1)S(1)}, u32[]{:S(2)}, u32[]{:S(2)}) collective-permute-start(bf16[32,512]{1,0:T(8,128)(2,1)S(1)} %get-tuple-element.493), channel_id=1, source_target_pairs={{0,1},{1,0},{2,3},{3,2},{4,5},{5,4},{6,7},{7,6},{8,9},{9,8},{10,11... | collective-permute-start | bytes 98312 | tf_op jit(solution)/shard_map/ppermute | solution.py:747
  49.4 0.7 collective-permute-start.8
  50.1 0.9 grads2.1
  51.0 8.2 %split.1 = (bf16[512,256]{1,0:T(8,128)(2,1)S(1)}, bf16[512,256]{1,0:T(8,128)(2,1)S(1)}, bf16[512,512]{1,0:T(8,128)(2,1)S(1)}, f32[512,512]{1,0:T(8,128)S(1)}, bf...) custom-call(s32[16]{0:T(128)S(1)} %get-tuple-element.362.refs_0_, ...), custom_call_target="tpu_custom_call", output_to_operand_aliasing={{10}: (14, {}), {11}: (15, {}), {12}: (16, {}), {13}: (17, ... | custom-call | flops 2904999936 | bytes 1 | tf_op jit(solution)/shard_map/split/pallas_call | solution.py:721
  59.2 3.6 %attback.3 = (f32[256,512]{1,0:T(8,128)S(1)}, bf16[512,512]{1,0:T(8,128)(2,1)S(1)}, bf16[512,256]{1,0:T(8,128)(2,1)S(1)}, bf16[512,256]{1,0:T(8,128)(2,1)S(1)}, ...) custom-call(s32[16]{0:T(128)S(1)} %get-tuple-element.362.refs_0_, ...), custom_call_target="tpu_custom_call", output_to_operand_aliasing={{2}: (7, {}), {3}: (8, {}), {4}: (9, {}), {5}: (10, {}), {6... | custom-call | flops 175000000 | bytes 1 | tf_op jit(solution)/shard_map/attback/pallas_call | solution.py:721
  62.8 3.6 %collective-permute-start.11 = (bf16[512,512]{1,0:T(8,128)(2,1)S(1)}, bf16[512,512]{1,0:T(8,128)(2,1)S(1)}, u32[]{:S(2)}, u32[]{:S(2)}) collective-permute-start(bf16[512,512]{1,0:T(8,128)(2,1)S(1)} %get-tuple-element.579), channel_id=1, source_target_pairs={{0,1},{1,0},{2,3},{3,2},{4,5},{5,4},{6,7},{7,6},{8,9},{9,8},{10,11... | collective-permute-start | bytes 1572872 | tf_op jit(solution)/shard_map/ppermute | solution.py:738
  66.4 0.1 collective-permute-start.9
  66.5 0.9 collective-permute-start.10
  67.4 0.6 collective-permute-done.9.refs_22_
  68.0 3.6 %attback.4 = (f32[256,512]{1,0:T(8,128)S(1)}, bf16[512,512]{1,0:T(8,128)(2,1)S(1)}, bf16[512,256]{1,0:T(8,128)(2,1)S(1)}, bf16[512,256]{1,0:T(8,128)(2,1)S(1)}, ...) custom-call(s32[16]{0:T(128)S(1)} %get-tuple-element.362.refs_0_, ...), custom_call_target="tpu_custom_call", output_to_operand_aliasing={{2}: (8, {}), {3}: (9, {}), {4}: (10, {}), {5}: (11, {}), {... | custom-call | flops 175000000 | bytes 1 | tf_op jit(solution)/shard_map/attback/pallas_call | solution.py:721
  71.6 0.2 join_kv.1
  71.8 6.4 %attback.5 = (f32[256,512]{1,0:T(8,128)S(1)}, bf16[512,512]{1,0:T(8,128)(2,1)S(1)}, f32[512,512]{1,0:T(8,128)S(1)}, bf16[512,256]{1,0:T(8,128)(2,1)S(1)}, bf16[5...) custom-call(s32[16]{0:T(128)S(1)} %get-tuple-element.362.refs_0_, ...), custom_call_target="tpu_custom_call", output_to_operand_aliasing={{3}: (9, {}), {4}: (10, {}), {5}: (11, {}), {6}: (12, {}), ... | custom-call | flops 2204999936 | bytes 1 | tf_op jit(solution)/shard_map/attback/pallas_call | solution.py:721
  78.2 4.2 %collective-permute-start.12 = (bf16[512,512]{1,0:T(8,128)(2,1)S(1)}, bf16[512,512]{1,0:T(8,128)(2,1)S(1)}, u32[]{:S(2)}, u32[]{:S(2)}) collective-permute-start(bf16[512,512]{1,0:T(8,128)(2,1)S(1)} %get-tuple-element.661), channel_id=1, source_target_pairs={{0,1},{1,0},{2,3},{3,2},{4,5},{5,4},{6,7},{7,6},{8,9},{9,8},{10,11... | collective-permute-start | bytes 1572872 | tf_op jit(solution)/shard_map/ppermute | solution.py:738
  82.4 1.7 collective-permute-start.13
  84.1 0.0 copy-start.15
  84.1 9.3 %gateback.1 = (f32[512,256]{1,0:T(8,128)S(1)}, f32[8,256]{1,0:T(8,128)S(1)}, f32[32,512]{1,0:T(8,128)S(1)}, f32[8,512]{1,0:T(8,128)S(1)}, bf16[1792,256]{1,0:T(8...) custom-call(s32[16]{0:T(128)S(1)} %get-tuple-element.362.refs_0_, ...), custom_call_target="tpu_custom_call", output_to_operand_aliasing={{5}: (19, {}), {6}: (20, {}), {7}: (21, {}), {8}: (22, {}),... | custom-call | flops 350000000 | bytes 1 | tf_op jit(solution)/shard_map/gateback/pallas_call | solution.py:721
  93.4 3.2 %collective-permute-done.13.refs_4_ = bf16[512,512]{1,0:T(8,128)(2,1)S(1)} collective-permute-done((bf16[512,512]{1,0:T(8,128)(2,1)S(1)}, bf16[512,512]{1,0:T(8,128)(2,1)S(1)}, u32[]{:S(2)}, u32[]{:S(2)}) %collective-permute-start.13) | collective-permute-done | bytes 524320 | tf_op jit(solution)/shard_map/ppermute | solution.py:738
  96.6 4.2 %last.1 = (f32[512,256]{1,0:T(8,128)}, f32[8,256]{1,0:T(8,128)S(1)}, bf16[2816,256]{1,0:T(8,128)(2,1)S(1)}, bf16[1792,256]{1,0:T(8,128)(2,1)S(1)}, f32[8,256]{1,...) custom-call(s32[16]{0:T(128)S(1)} %get-tuple-element.362.refs_0_, ...), custom_call_target="tpu_custom_call", output_to_operand_aliasing={{3}: (18, {}), {4}: (19, {}), {5}: (20, {}), {6}: (21, {}),... | custom-call | flops 1470000000 | bytes 1 | tf_op jit(solution)/shard_map/last/pallas_call | solution.py:721
  100.8 0.3 pack.1
  101.1 0.1 collective-permute-start.14
  101.2 4.0 %collective-permute-done.14.got = bf16[3840,256]{1,0:T(8,128)(2,1)S(1)} collective-permute-done((bf16[3840,256]{1,0:T(8,128)(2,1)S(1)}, bf16[3840,256]{1,0:T(8,128)(2,1)S(1)}, u32[]{:S(2)}, u32[]{:S(2)}) %collective-permute-start.14) | collective-permute-done | bytes 1966112 | tf_op jit(solution)/shard_map/ppermute | solution.py:668
  105.2 0.4 shard_map.325
  105.6 1.8 collective-permute-start.15
  107.4 12.3 %collective-permute-done.15.got = bf16[1920,256]{1,0:T(8,128)(2,1)S(1)} collective-permute-done((bf16[1920,256]{1,0:T(8,128)(2,1)S(1)}, bf16[1920,256]{1,0:T(8,128)(2,1)S(1)}, u32[]{:S(2)}, u32[]{:S(2)}) %collective-permute-start.15) | collective-permute-done | bytes 983072 | tf_op jit(solution)/shard_map/ppermute | solution.py:668
  119.8 0.2 shard_map.326
  120.0 0.1 collective-permute-start.16
  120.1 8.8 %collective-permute-done.16.got = bf16[960,256]{1,0:T(8,128)(2,1)S(1)} collective-permute-done((bf16[960,256]{1,0:T(8,128)(2,1)S(1)}, bf16[960,256]{1,0:T(8,128)(2,1)S(1)}, u32[]{:S(2)}, u32[]{:S(2)}) %collective-permute-start.16) | collective-permute-done | bytes 491552 | tf_op jit(solution)/shard_map/ppermute | solution.py:668
  128.9 0.1 shard_map.327
  129.0 1.6 collective-permute-start.17
  130.6 4.7 %collective-permute-done.17.got = bf16[480,256]{1,0:T(8,128)(2,1)S(1)} collective-permute-done((bf16[480,256]{1,0:T(8,128)(2,1)S(1)}, bf16[480,256]{1,0:T(8,128)(2,1)S(1)}, u32[]{:S(2)}, u32[]{:S(2)}) %collective-permute-start.17) | collective-permute-done | bytes 245792 | tf_op jit(solution)/shard_map/ppermute | solution.py:668
  135.3 0.1 shard_map.328
  135.3 2.7 %collective-permute-start.18 = (bf16[240,256]{1,0:T(8,128)(2,1)S(1)}, bf16[240,256]{1,0:T(8,128)(2,1)S(1)}, u32[]{:S(2)}, u32[]{:S(2)}) collective-permute-start(bf16[240,256]{1,0:T(8,128)(2,1)S(1)} %get-tuple-element.695), channel_id=1, source_target_pairs={{0,16},{1,17},{2,18},{3,19},{4,20},{5,21},{6,22},{7,23},{8,24},{9,... | collective-permute-start | bytes 368648 | tf_op jit(solution)/shard_map/ppermute | solution.py:668
  138.0 4.5 %collective-permute-done.18.got = bf16[240,256]{1,0:T(8,128)(2,1)S(1)} collective-permute-done((bf16[240,256]{1,0:T(8,128)(2,1)S(1)}, bf16[240,256]{1,0:T(8,128)(2,1)S(1)}, u32[]{:S(2)}, u32[]{:S(2)}) %collective-permute-start.18) | collective-permute-done | bytes 122912 | tf_op jit(solution)/shard_map/ppermute | solution.py:668
  142.5 1.4 collective-permute-start.19
  144.0 4.5 %collective-permute-done.19.got = bf16[240,256]{1,0:T(8,128)(2,1)S(1)} collective-permute-done((bf16[240,256]{1,0:T(8,128)(2,1)S(1)}, bf16[240,256]{1,0:T(8,128)(2,1)S(1)}, u32[]{:S(2)}, u32[]{:S(2)}) %collective-permute-start.19) | collective-permute-done | bytes 122912 | tf_op jit(solution)/shard_map/ppermute | solution.py:668
  148.5 1.6 collective-permute-start.20
  150.1 4.7 %collective-permute-done.20.got = bf16[480,256]{1,0:T(8,128)(2,1)S(1)} collective-permute-done((bf16[480,256]{1,0:T(8,128)(2,1)S(1)}, bf16[480,256]{1,0:T(8,128)(2,1)S(1)}, u32[]{:S(2)}, u32[]{:S(2)}) %collective-permute-start.20) | collective-permute-done | bytes 245792 | tf_op jit(solution)/shard_map/ppermute | solution.py:668
  154.8 0.1 shard_map.331.mine
  154.8 4.9 %collective-permute-start.21 = (bf16[960,256]{1,0:T(8,128)(2,1)S(1)}, bf16[960,256]{1,0:T(8,128)(2,1)S(1)}, u32[]{:S(2)}, u32[]{:S(2)}) collective-permute-start(bf16[960,256]{1,0:T(8,128)(2,1)S(1)} %shard_map.331.mine), channel_id=1, source_target_pairs={{0,8},{1,3},{2,10},{3,1},{4,12},{5,7},{6,14},{7,5},{8,0},{9,11},{1... | collective-permute-start | bytes 1474568 | tf_op jit(solution)/shard_map/ppermute | solution.py:668
  159.7 6.8 %collective-permute-done.21.got = bf16[960,256]{1,0:T(8,128)(2,1)S(1)} collective-permute-done((bf16[960,256]{1,0:T(8,128)(2,1)S(1)}, bf16[960,256]{1,0:T(8,128)(2,1)S(1)}, u32[]{:S(2)}, u32[]{:S(2)}) %collective-permute-start.21) | collective-permute-done | bytes 491552 | tf_op jit(solution)/shard_map/ppermute | solution.py:668
  166.5 0.1 shard_map.332.mine
  166.6 1.8 collective-permute-start.22
  168.5 12.3 %collective-permute-done.22.got = bf16[1920,256]{1,0:T(8,128)(2,1)S(1)} collective-permute-done((bf16[1920,256]{1,0:T(8,128)(2,1)S(1)}, bf16[1920,256]{1,0:T(8,128)(2,1)S(1)}, u32[]{:S(2)}, u32[]{:S(2)}) %collective-permute-start.22) | collective-permute-done | bytes 983072 | tf_op jit(solution)/shard_map/ppermute | solution.py:668
  180.8 0.2 shard_map.333.mine
  181.0 0.1 collective-permute-start.23
  181.1 4.0 %collective-permute-done.23.got = bf16[3840,256]{1,0:T(8,128)(2,1)S(1)} collective-permute-done((bf16[3840,256]{1,0:T(8,128)(2,1)S(1)}, bf16[3840,256]{1,0:T(8,128)(2,1)S(1)}, u32[]{:S(2)}, u32[]{:S(2)}) %collective-permute-start.23) | collective-permute-done | bytes 1966112 | tf_op jit(solution)/shard_map/ppermute | solution.py:668
  185.0 3.5 %shard_map.334 = (f32[5,256]{1,0:T(8,128)}, f32[1,512]{1,0:T(1,128)}, f32[256,1024]{1,0:T(8,128)}, f32[1024,256]{1,0:T(8,128)}, f32[256,768]{1,0:T(8,128)}, /*in...) custom-call(bf16[3840,256]{1,0:T(8,128)(2,1)S(1)} %shard_map.333.min, ...), custom_call_target="tpu_custom_call" | custom-call | flops 1050000000 | bytes 1 | tf_op jit(solution)/shard_map/pallas_call | solution.py:644
  (42 shorter events, 0.2 us)
Async XLA Ops:
  1.3 7.2 %copy-start = (bf16[256,1024]{1,0:T(8,128)(2,1)S(1)}, bf16[256,1024]{1,0:T(8,128)(2,1)}, u32[]{:S(2)}) copy-start(bf16[256,1024]{1,0:T(8,128)(2,1)} %refs_17_.2) | copy-start | bytes 1572868
  1.3 7.2 %copy-start.13 = (f32[5,256]{1,0:T(8,128)S(1)}, f32[5,256]{1,0:T(8,128)}, u32[]{:S(2)}) copy-start(f32[5,256]{1,0:T(8,128)} %refs_14_.1) | copy-start | bytes 15364
  1.3 7.2 %copy-start.14 = (f32[512]{0:T(512)S(1)}, f32[512]{0:T(512)}, u32[]{:S(2)}) copy-start(f32[512]{0:T(512)} %param.31) | copy-start | bytes 6148
  5.5 7.0 %collective-permute-start = (bf16[512,512]{1,0:T(8,128)(2,1)S(1)}, bf16[512,512]{1,0:T(8,128)(2,1)S(1)}, u32[]{:S(2)}, u32[]{:S(2)}) collective-permute-start(bf16[512,512]{1,0:T(8,128)(2,1)S(1)} %get-tuple-element.372), channel_id=1, source_target_pairs={{0,1},{1,0},{2,3},{3,2},{4,5},{5,4},{6,7},{7,6},{8,9},{9,8},{10,11... | collective-permute-start | bytes 1572872 | tf_op jit(solution)/shard_map/ppermute | solution.py:738
  6.0 17.5 %collective-permute-start.3 = (bf16[512,512]{1,0:T(8,128)(2,1)S(1)}, bf16[512,512]{1,0:T(8,128)(2,1)S(1)}, u32[]{:S(2)}, u32[]{:S(2)}) collective-permute-start(bf16[512,512]{1,0:T(8,128)(2,1)S(1)} %get-tuple-element.372), channel_id=1, source_target_pairs={{0,2},{1,3},{2,0},{3,1},{4,6},{5,7},{6,4},{7,5},{8,10},{9,11},{10,... | collective-permute-start | bytes 1572872 | tf_op jit(solution)/shard_map/ppermute | solution.py:738
  11.0 6.7 %collective-permute-start.1 = (bf16[32,512]{1,0:T(8,128)(2,1)S(1)}, bf16[32,512]{1,0:T(8,128)(2,1)S(1)}, u32[]{:S(2)}, u32[]{:S(2)}) collective-permute-start(bf16[32,512]{1,0:T(8,128)(2,1)S(1)} %get-tuple-element.384), channel_id=1, source_target_pairs={{0,1},{1,0},{2,3},{3,2},{4,5},{5,4},{6,7},{7,6},{8,9},{9,8},{10,11... | collective-permute-start | bytes 98312 | tf_op jit(solution)/shard_map/ppermute | solution.py:747
  11.3 6.4 %collective-permute-start.2 = (bf16[32,512]{1,0:T(8,128)(2,1)S(1)}, bf16[32,512]{1,0:T(8,128)(2,1)S(1)}, u32[]{:S(2)}, u32[]{:S(2)}) collective-permute-start(bf16[32,512]{1,0:T(8,128)(2,1)S(1)} %get-tuple-element.385), channel_id=1, source_target_pairs={{1,2},{2,1},{5,6},{6,5},{9,10},{10,9},{13,14},{14,13},{17,18},{18,... | collective-permute-start | bytes 98312 | tf_op jit(solution)/shard_map/ppermute | solution.py:747
  12.5 5.3 %copy-start.1 = (bf16[512,256]{1,0:T(8,128)(2,1)S(1)}, bf16[512,256]{1,0:T(8,128)(2,1)}, u32[]{:S(2)}) copy-start(bf16[512,256]{1,0:T(8,128)(2,1)} %refs_12_.2) | copy-start | bytes 786436
  12.5 5.2 %copy-start.12 = (bf16[31,512]{1,0:T(8,128)(2,1)S(1)}, bf16[31,512]{1,0:T(8,128)(2,1)}, u32[]{:S(2)}) copy-start(bf16[31,512]{1,0:T(8,128)(2,1)} %refs_15_.2) | copy-start | bytes 95236
  23.4 6.5 %collective-permute-start.4 = (bf16[512,512]{1,0:T(8,128)(2,1)S(1)}, bf16[512,512]{1,0:T(8,128)(2,1)S(1)}, u32[]{:S(2)}, u32[]{:S(2)}) collective-permute-start(bf16[512,512]{1,0:T(8,128)(2,1)S(1)} %collective-permute-done.3.refs_2_.refs_16_), channel_id=1, source_target_pairs={{0,1},{1,0},{2,3},{3,2},{4,5},{5,4},{6,7},{7,6},{8,9},{9,8},{10,11... | collective-permute-start | bytes 1572872 | tf_op jit(solution)/shard_map/ppermute | solution.py:738
  27.0 2.9 %copy-start.2 = (bf16[256,256]{1,0:T(8,128)(2,1)S(1)}, bf16[256,256]{1,0:T(8,128)(2,1)}, u32[]{:S(2)}) copy-start(bf16[256,256]{1,0:T(8,128)(2,1)} %refs_13_.2) | copy-start | bytes 393220
  29.9 4.7 %copy-start.3 = (f32[512,256]{1,0:T(8,128)S(1)}, f32[512,256]{1,0:T(8,128)}, u32[]{:S(2)}) copy-start(f32[512,256]{1,0:T(8,128)} %refs_8_.3) | copy-start | bytes 1572868
  29.9 4.7 %copy-start.4 = (bf16[256,1024]{1,0:T(8,128)(2,1)S(1)}, bf16[256,1024]{1,0:T(8,128)(2,1)}, u32[]{:S(2)}) copy-start(bf16[256,1024]{1,0:T(8,128)(2,1)} %refs_10_.3) | copy-start | bytes 1572868
  30.0 4.7 %copy-start.5 = (bf16[1024,256]{1,0:T(8,128)(2,1)S(1)}, bf16[1024,256]{1,0:T(8,128)(2,1)}, u32[]{:S(2)}) copy-start(bf16[1024,256]{1,0:T(8,128)(2,1)} %refs_11_.4) | copy-start | bytes 1572868
  30.0 4.7 %copy-start.9 = (bf16[512,256]{1,0:T(8,128)(2,1)S(1)}, bf16[512,256]{1,0:T(8,128)(2,1)}, u32[]{:S(2)}) copy-start(bf16[512,256]{1,0:T(8,128)(2,1)} %refs_7_.4) | copy-start | bytes 786436
  30.0 4.7 %copy-start.11 = (bf16[31,512]{1,0:T(8,128)(2,1)S(1)}, bf16[31,512]{1,0:T(8,128)(2,1)}, u32[]{:S(2)}) copy-start(bf16[31,512]{1,0:T(8,128)(2,1)} %refs_11_.5) | copy-start | bytes 95236
  33.4 1.3 collective-permute-start.5
  33.5 1.2 collective-permute-start.6
  44.7 6.3 %collective-permute-start.7 = (bf16[32,512]{1,0:T(8,128)(2,1)S(1)}, bf16[32,512]{1,0:T(8,128)(2,1)S(1)}, u32[]{:S(2)}, u32[]{:S(2)}) collective-permute-start(bf16[32,512]{1,0:T(8,128)(2,1)S(1)} %get-tuple-element.493), channel_id=1, source_target_pairs={{0,1},{1,0},{2,3},{3,2},{4,5},{5,4},{6,7},{7,6},{8,9},{9,8},{10,11... | collective-permute-start | bytes 98312 | tf_op jit(solution)/shard_map/ppermute | solution.py:747
  49.4 1.6 collective-permute-start.8
  62.8 8.8 %collective-permute-start.11 = (bf16[512,512]{1,0:T(8,128)(2,1)S(1)}, bf16[512,512]{1,0:T(8,128)(2,1)S(1)}, u32[]{:S(2)}, u32[]{:S(2)}) collective-permute-start(bf16[512,512]{1,0:T(8,128)(2,1)S(1)} %get-tuple-element.579), channel_id=1, source_target_pairs={{0,1},{1,0},{2,3},{3,2},{4,5},{5,4},{6,7},{7,6},{8,9},{9,8},{10,11... | collective-permute-start | bytes 1572872 | tf_op jit(solution)/shard_map/ppermute | solution.py:738
  66.4 1.6 collective-permute-start.9
  66.5 1.5 collective-permute-start.10
  78.2 15.2 %collective-permute-start.12 = (bf16[512,512]{1,0:T(8,128)(2,1)S(1)}, bf16[512,512]{1,0:T(8,128)(2,1)S(1)}, u32[]{:S(2)}, u32[]{:S(2)}) collective-permute-start(bf16[512,512]{1,0:T(8,128)(2,1)S(1)} %get-tuple-element.661), channel_id=1, source_target_pairs={{0,1},{1,0},{2,3},{3,2},{4,5},{5,4},{6,7},{7,6},{8,9},{9,8},{10,11... | collective-permute-start | bytes 1572872 | tf_op jit(solution)/shard_map/ppermute | solution.py:738
  82.4 14.2 %collective-permute-start.13 = (bf16[512,512]{1,0:T(8,128)(2,1)S(1)}, bf16[512,512]{1,0:T(8,128)(2,1)S(1)}, u32[]{:S(2)}, u32[]{:S(2)}) collective-permute-start(bf16[512,512]{1,0:T(8,128)(2,1)S(1)} %get-tuple-element.662), channel_id=1, source_target_pairs={{0,2},{1,3},{2,0},{3,1},{4,6},{5,7},{6,4},{7,5},{8,10},{9,11},{10,... | collective-permute-start | bytes 1572872 | tf_op jit(solution)/shard_map/ppermute | solution.py:738
  84.1 12.5 %copy-start.6 = (bf16[256,1024]{1,0:T(8,128)(2,1)S(1)}, bf16[256,1024]{1,0:T(8,128)(2,1)}, u32[]{:S(2)}) copy-start(bf16[256,1024]{1,0:T(8,128)(2,1)} %refs_16_.1) | copy-start | bytes 1572868
  84.1 12.5 %copy-start.7 = (bf16[1024,256]{1,0:T(8,128)(2,1)S(1)}, bf16[1024,256]{1,0:T(8,128)(2,1)}, u32[]{:S(2)}) copy-start(bf16[1024,256]{1,0:T(8,128)(2,1)} %refs_17_.3) | copy-start | bytes 1572868
  84.1 12.5 %copy-start.8 = (bf16[256,768]{1,0:T(8,128)(2,1)S(1)}, bf16[256,768]{1,0:T(8,128)(2,1)}, u32[]{:S(2)}) copy-start(bf16[256,768]{1,0:T(8,128)(2,1)} %refs_13_.3) | copy-start | bytes 1179652
  84.1 12.5 %copy-start.10 = (bf16[512,256]{1,0:T(8,128)(2,1)S(1)}, bf16[512,256]{1,0:T(8,128)(2,1)}, u32[]{:S(2)}) copy-start(bf16[512,256]{1,0:T(8,128)(2,1)} %refs_15_.3) | copy-start | bytes 786436
  84.1 12.5 %copy-start.15 = (f32[1,128]{1,0:T(1,128)S(1)}, f32[1,128]{1,0:T(1,128)}, u32[]{:S(2)}) copy-start(f32[1,128]{1,0:T(1,128)} %constant.2.clone.refs_7_.refs_12_) | copy-start | bytes 1540
  101.1 4.0 %collective-permute-start.14 = (bf16[3840,256]{1,0:T(8,128)(2,1)S(1)}, bf16[3840,256]{1,0:T(8,128)(2,1)S(1)}, u32[]{:S(2)}, u32[]{:S(2)}) collective-permute-start(bf16[3840,256]{1,0:T(8,128)(2,1)S(1)} %get-tuple-element.687), channel_id=1, source_target_pairs={{0,1},{1,0},{2,3},{3,2},{4,5},{5,4},{6,7},{7,6},{8,9},{9,8},{10,11... | collective-permute-start | bytes 5898248 | tf_op jit(solution)/shard_map/ppermute | solution.py:668
  105.6 14.2 %collective-permute-start.15 = (bf16[1920,256]{1,0:T(8,128)(2,1)S(1)}, bf16[1920,256]{1,0:T(8,128)(2,1)S(1)}, u32[]{:S(2)}, u32[]{:S(2)}) collective-permute-start(bf16[1920,256]{1,0:T(8,128)(2,1)S(1)} %get-tuple-element.689), channel_id=1, source_target_pairs={{0,2},{1,5},{2,0},{3,7},{4,6},{5,1},{6,4},{7,3},{8,10},{9,13},{10,... | collective-permute-start | bytes 2949128 | tf_op jit(solution)/shard_map/ppermute | solution.py:668
  120.0 8.9 %collective-permute-start.16 = (bf16[960,256]{1,0:T(8,128)(2,1)S(1)}, bf16[960,256]{1,0:T(8,128)(2,1)S(1)}, u32[]{:S(2)}, u32[]{:S(2)}) collective-permute-start(bf16[960,256]{1,0:T(8,128)(2,1)S(1)} %get-tuple-element.691), channel_id=1, source_target_pairs={{0,8},{1,3},{2,10},{3,1},{4,12},{5,7},{6,14},{7,5},{8,0},{9,11},{1... | collective-permute-start | bytes 1474568 | tf_op jit(solution)/shard_map/ppermute | solution.py:668
  129.0 6.3 %collective-permute-start.17 = (bf16[480,256]{1,0:T(8,128)(2,1)S(1)}, bf16[480,256]{1,0:T(8,128)(2,1)S(1)}, u32[]{:S(2)}, u32[]{:S(2)}) collective-permute-start(bf16[480,256]{1,0:T(8,128)(2,1)S(1)} %get-tuple-element.693), channel_id=1, source_target_pairs={{0,4},{1,9},{2,6},{3,11},{4,0},{5,13},{6,2},{7,15},{8,12},{9,1},{1... | collective-permute-start | bytes 737288 | tf_op jit(solution)/shard_map/ppermute | solution.py:668
  135.3 7.2 %collective-permute-start.18 = (bf16[240,256]{1,0:T(8,128)(2,1)S(1)}, bf16[240,256]{1,0:T(8,128)(2,1)S(1)}, u32[]{:S(2)}, u32[]{:S(2)}) collective-permute-start(bf16[240,256]{1,0:T(8,128)(2,1)S(1)} %get-tuple-element.695), channel_id=1, source_target_pairs={{0,16},{1,17},{2,18},{3,19},{4,20},{5,21},{6,22},{7,23},{8,24},{9,... | collective-permute-start | bytes 368648 | tf_op jit(solution)/shard_map/ppermute | solution.py:668
  142.5 5.9 %collective-permute-start.19 = (bf16[240,256]{1,0:T(8,128)(2,1)S(1)}, bf16[240,256]{1,0:T(8,128)(2,1)S(1)}, u32[]{:S(2)}, u32[]{:S(2)}) collective-permute-start(bf16[240,256]{1,0:T(8,128)(2,1)S(1)} %shard_map.329.mine), channel_id=1, source_target_pairs={{0,16},{1,17},{2,18},{3,19},{4,20},{5,21},{6,22},{7,23},{8,24},{9,... | collective-permute-start | bytes 368648 | tf_op jit(solution)/shard_map/ppermute | solution.py:668
  148.5 6.3 %collective-permute-start.20 = (bf16[480,256]{1,0:T(8,128)(2,1)S(1)}, bf16[480,256]{1,0:T(8,128)(2,1)S(1)}, u32[]{:S(2)}, u32[]{:S(2)}) collective-permute-start(bf16[480,256]{1,0:T(8,128)(2,1)S(1)} %shard_map.330.mine), channel_id=1, source_target_pairs={{0,4},{1,9},{2,6},{3,11},{4,0},{5,13},{6,2},{7,15},{8,12},{9,1},{1... | collective-permute-start | bytes 737288 | tf_op jit(solution)/shard_map/ppermute | solution.py:668
  154.8 11.7 %collective-permute-start.21 = (bf16[960,256]{1,0:T(8,128)(2,1)S(1)}, bf16[960,256]{1,0:T(8,128)(2,1)S(1)}, u32[]{:S(2)}, u32[]{:S(2)}) collective-permute-start(bf16[960,256]{1,0:T(8,128)(2,1)S(1)} %shard_map.331.mine), channel_id=1, source_target_pairs={{0,8},{1,3},{2,10},{3,1},{4,12},{5,7},{6,14},{7,5},{8,0},{9,11},{1... | collective-permute-start | bytes 1474568 | tf_op jit(solution)/shard_map/ppermute | solution.py:668
  166.6 14.2 %collective-permute-start.22 = (bf16[1920,256]{1,0:T(8,128)(2,1)S(1)}, bf16[1920,256]{1,0:T(8,128)(2,1)S(1)}, u32[]{:S(2)}, u32[]{:S(2)}) collective-permute-start(bf16[1920,256]{1,0:T(8,128)(2,1)S(1)} %shard_map.332.mine), channel_id=1, source_target_pairs={{0,2},{1,5},{2,0},{3,7},{4,6},{5,1},{6,4},{7,3},{8,10},{9,13},{10,... | collective-permute-start | bytes 2949128 | tf_op jit(solution)/shard_map/ppermute | solution.py:668
  181.0 4.0 %collective-permute-start.23 = (bf16[3840,256]{1,0:T(8,128)(2,1)S(1)}, bf16[3840,256]{1,0:T(8,128)(2,1)S(1)}, u32[]{:S(2)}, u32[]{:S(2)}) collective-permute-start(bf16[3840,256]{1,0:T(8,128)(2,1)S(1)} %shard_map.333.mine), channel_id=1, source_target_pairs={{0,1},{1,0},{2,3},{3,2},{4,5},{5,4},{6,7},{7,6},{8,9},{9,8},{10,11... | collective-permute-start | bytes 5898248 | tf_op jit(solution)/shard_map/ppermute | solution.py:668
